TPU v7x, 32 devices: a whole 2x2x4 slice. The times are simulated.
32 devices in a mesh: row: 8 (over z, core), col: 4 (over y, x).
Axes of the slice: x: 2, y: 2, z: 4, core: 2. Of those that a mesh axis runs over, the one named last changes fastest.
Arguments:
- spans: bfloat16 [4096, 768], P(('row', 'col')), may hold values from -10 to 10
- centroids: bfloat16 [2048, 768], P(('col', 'row')), may hold values from -10 to 10
- pattern: int32 [32, 4], P('row'), may hold values from 0 to 15, as said below
Outputs:
- new_centroids: bfloat16 [2048, 768], P(('col', 'row'))
- row_potential: float32 [4096], P('row')
- col_potential: float32 [2048], P('col')
Inputs may be any that keep to these rules, and one draw needn't show every extreme that they name: `pattern`: each row lists 4 distinct centroid blocks in rising order; row b always lists block b % 16; every centroid block is listed by some row.
All inputs are finite; a program needn't handle non-finite values.
Results may differ from a plain program's by a relative error of at most 0.0095.
Values may be sent and summed in bfloat16 or wider, within the bound.
No kernel may reach another device: no remote copies, remote signals or barrier semaphores. Data moves between devices by JAX's collectives and lax.ppermute only.
A program may use at most 64 MiB of HBM per device.

v0:
```python
import math

import jax
import jax.numpy as jnp
from jax import lax
from jax.sharding import PartitionSpec as P

ITERS = 3


logit_scale = 0.0625
floor_value = -1e30


def swap(x, axis, k):
    return lax.ppermute(x, axis, [(i, i ^ k) for i in range(lax.axis_size(axis))])


def swap_by_core(x, axis, for_core):
    cols = lax.axis_size("col")
    scale = cols if axis == "row" else 1
    pairs = [(i, i ^ (for_core[i // cols & 1] * scale)) for i in range(lax.axis_size("row") * cols)]
    return lax.ppermute(x, ("row", "col"), pairs)


def stages(axis):
    low = 1 if axis == "row" else 0
    bits = (lax.axis_size(axis) - 1).bit_length()
    return [(at, 1 << min(2, bits - at)) for at in range(low, bits, 2)]


def digit(axis, at, size):
    return (lax.axis_index(axis) >> at) & (size - 1)


def gather_spans(x, core):
    first = None
    parts = [x]
    ready = x
    for at, size in stages("col"):
        x = jnp.concatenate(parts)
        parts = [x] + [swap(x, "col", d << at) for d in range(1, min(size, 3))]
        first = parts[1] if first is None else first
        near = parts
        if size == 4:
            passed_on = jnp.where(core == 1, parts[2], parts[1])
            near = lax.optimization_barrier((parts, passed_on))[0]
            ready = passed_on
            parts = parts + [swap_by_core(passed_on, "col", (2 << at, 1 << at))]
    mate = [swap(part, "row", 1) for part in near + parts[3:]]
    return parts, mate, first, ready


def after(x, other):
    return lax.optimization_barrier((x, other))[0]


def placed(parts, index):
    whole = jnp.zeros((len(parts),) + parts[0].shape, parts[0].dtype)
    for d, part in enumerate(parts):
        whole = lax.dynamic_update_index_in_dim(whole, part, index ^ d, 0)
    return whole.reshape((-1,) + parts[0].shape[1:])


def gather_centroids(x, first, ready):
    for at, size in stages("row"):
        parts = [x] + [swap(after(x, first) if d << at == 2 else x, "row", d << at) for d in range(1, size)]
        mate = [swap(after(part, ready), "row", 1) for part in parts]
        position = digit("row", at, size)
        x = placed(parts, position)
    return jnp.concatenate([x, placed(mate, position)])


def reorder(x, blocks, k):
    x = x.reshape((blocks, -1) + x.shape[1:])
    return jnp.concatenate([x[p ^ k] for p in range(blocks)])


def unxor(x, index, blocks):
    shape = x.shape
    bit = 1
    while bit < blocks:
        pairs = x.reshape((blocks // (2 * bit), 2, -1) + shape[1:])
        x = jnp.where((index & bit) != 0, pairs[:, ::-1], pairs).reshape(shape)
        bit *= 2
    return x


def tree(op, parts):
    while len(parts) > 1:
        parts = [op(parts[i], parts[i + 1]) for i in range(0, len(parts), 2)]
    return parts[0]


def add(parts):
    return tree(jnp.add, parts)


def log_sum(parts):
    high = tree(jnp.maximum, parts)
    return high + jnp.log(add([jnp.exp(part - high) for part in parts]))


def over_rows(merge, x):
    for at, size in stages("row"):
        x = merge([x] + [swap(x, "row", d << at) for d in range(1, size)])
    return x


def over_cols(merge, x):
    cols = lax.axis_size("col")
    for at, size in stages("col"):
        parts = [x]
        for d in range(1, size):
            halves = swap(x, "col", d << at).reshape(2, -1)
            parts.append(jnp.concatenate([reorder(half, cols, d << at) for half in halves]))
        x = merge(parts)
    return x


def in_thirds(x, width):
    thirds = []
    for step in range(3):
        top = lax.reduce_precision(x, 8, 7)
        thirds.append(top.astype(jnp.bfloat16))
        x = x - top
    return jnp.pad(jnp.stack(thirds), ((0, 5), (0, width - x.shape[0])))


def from_thirds(rows, count):
    thirds = rows[:3, :count].astype(jnp.float32)
    return thirds[0] + thirds[1] + thirds[2]


def per_device(spans, centroids, pattern):
    rows, cols = lax.axis_size("row"), lax.axis_size("col")
    chips = rows // 2
    me_row, me_col = lax.axis_index("row"), lax.axis_index("col")
    core = me_row % 2
    per, width = centroids.shape
    half_cols = per * chips
    group_cols = 2 * half_cols
    row_count = spans.shape[0] * cols
    mass_ratio = group_cols * cols / (row_count * rows)
    target = 1 / mass_ratio

    mate_pattern = swap(pattern, "row", 1)
    own_parts, mate_parts, first, ready = gather_spans(spans, core)
    tile_centroids = gather_centroids(centroids, first, ready)
    span_halves = [jnp.concatenate(own_parts), jnp.concatenate(mate_parts)]
    at = jnp.arange(group_cols)
    row_of = at % half_cols // per * 2 + (at // half_cols ^ core)
    blocks = jnp.arange(group_cols // 128)
    in_block = ((row_of * per + at % per) // 128 == blocks[:, None]).astype(jnp.bfloat16)

    def half_scores(lists, span_half):
        listed = jnp.any(lists[:, :, None] == me_col * blocks.shape[0] + blocks, axis=1)
        listed = unxor(jnp.repeat(listed, 128 // spans.shape[0], axis=0).astype(jnp.bfloat16), me_col, cols)
        allowed_cells = jnp.dot(
            jnp.repeat(listed, spans.shape[0], axis=0), in_block, preferred_element_type=jnp.float32
        )
        products = lax.dot_general(
            span_half, tile_centroids, (((1,), (1,)), ((), ())), preferred_element_type=jnp.float32
        )
        return jnp.where(allowed_cells > 0.5, products * logit_scale, floor_value)

    scores = [half_scores(pattern, span_halves[0]), half_scores(mate_pattern, span_halves[1])]

    def with_rows(row_pot):
        return [half + row_pot[n * row_count : (n + 1) * row_count, None] for n, half in enumerate(scores)]

    def row_sums(row_pot, col_pot):
        return jnp.concatenate([jnp.sum(jnp.exp(x + col_pot[None, :]), axis=1) for x in with_rows(row_pot)])

    def col_sums(row_pot, col_pot):
        return add([jnp.sum(jnp.exp(x + col_pot[None, :]), axis=0) for x in with_rows(row_pot)])

    def rounds():
        highs = [jnp.max(half, axis=1) for half in scores]
        totals = [jnp.sum(jnp.exp(half - high[:, None]), axis=1) for half, high in zip(scores, highs)]
        row_pot = -over_cols(log_sum, jnp.concatenate([high + jnp.log(total) for high, total in zip(highs, totals)]))
        high = tree(jnp.maximum, [jnp.max(x, axis=0) for x in with_rows(row_pot)])
        total = col_sums(row_pot, -high)
        col_pot = math.log(target) - over_rows(log_sum, high + jnp.log(total))
        for sweep in range(1, ITERS):
            row_pot = row_pot - jnp.log(over_cols(add, row_sums(row_pot, col_pot)))
            if sweep < ITERS - 1:
                mass = over_rows(add, col_sums(row_pot, col_pot))
                col_pot = col_pot + math.log(target) - jnp.log(mass)
        return jnp.concatenate([row_pot.reshape(-1, group_cols), col_pot[None]])

    def nothing():
        return jnp.zeros((2 * row_count // group_cols + 1, group_cols), jnp.float32)

    known = lax.cond(core == 1, rounds, nothing)
    got = swap(known, "row", 1)
    row_pot = jnp.where(core == 1, known[:-1].reshape(-1), reorder(got[:-1].reshape(-1), 2, 1))
    col_pot = jnp.where(core == 1, known[-1], reorder(got[-1], 2, 1))

    mass = col_sums(row_pot, col_pot)
    held = add(
        [
            lax.dot_general(
                jnp.exp(x[:, :half_cols] + col_pot[None, :half_cols]).astype(jnp.bfloat16),
                span_half,
                (((0,), (0,)), ((), ())),
                preferred_element_type=jnp.float32,
            )
            for x, span_half in zip(with_rows(row_pot), span_halves)
        ]
    ).reshape(chips, per, width)
    for at, size in stages("row"):
        me = digit("row", at, size)
        held = held.reshape((-1, size) + held.shape[1:])
        low = held.astype(jnp.bfloat16)
        note = in_thirds(mass, width)
        parts, masses = [lax.dynamic_index_in_dim(held, me, 1, keepdims=False)], [from_thirds(note, group_cols)]
        for d in range(1, size):
            block = lax.dynamic_index_in_dim(low, me ^ d, 1, keepdims=False).reshape(-1, width)
            got = swap(jnp.concatenate([block, note]), "row", d << at)
            if d << at == 2:
                row_out = unxor(after(row_pot[:row_count], got), me_col, cols)
            parts.append(got[: block.shape[0]].astype(jnp.float32).reshape(parts[0].shape))
            masses.append(from_thirds(got[block.shape[0] :], group_cols))
        held, mass = add(parts), add(masses)
    own_mass = lax.dynamic_slice_in_dim(mass, me_row // 2 * per, per, 0)
    col_pots = (col_pot + math.log(target) - jnp.log(mass)).reshape(2, chips, per)
    col_pots = jnp.where(core == 1, col_pots[::-1], col_pots)
    return (
        (held.reshape(per, width) * (target * mass_ratio / own_mass)[:, None]).astype(jnp.bfloat16),
        row_out,
        col_pots.swapaxes(0, 1).reshape(-1),
    )


def solution(mesh):
    placed = (P(("row", "col"), None), P(("col", "row"), None), P("row", None))
    return jax.shard_map(
        per_device,
        mesh=mesh,
        in_specs=placed,
        out_specs=(P(("col", "row"), None), P("row"), P("col")),
        check_vma=False,
    )
```

profile of v0, /device:TPU:0, one launch (start us, length us, event | category | flops | bytes accessed | tf_op | source)
XLA Modules:
  0.0 70.9 jit_solution(4240666507296470279)
XLA Ops:
  0.6 4.1 %collective-permute-start.19 = (bf16[64,768]{1,0:T(8,128)(2,1)}, bf16[64,768]{1,0:T(8,128)(2,1)S(1)}, u32[]{:S(2)}, u32[]{:S(2)}) collective-permute-start(bf16[64,768]{1,0:T(8,128)(2,1)} %param.6), channel_id=1, source_target_pairs={{0,16},{4,20},{8,24},{12,28},{16,0},{20,4},{24,8},{28,12},{1,17},{... | collective-permute-start | bytes 294920 | tf_op jit(solution)/shard_map/ppermute | solution.py:16
  4.7 1.3 %collective-permute-start.20 = (bf16[64,768]{1,0:T(8,128)(2,1)}, bf16[64,768]{1,0:T(8,128)(2,1)S(1)}, u32[]{:S(2)}, u32[]{:S(2)}) collective-permute-start(bf16[64,768]{1,0:T(8,128)(2,1)} %param.6), channel_id=1, source_target_pairs={{0,24},{4,28},{8,16},{12,20},{16,8},{20,12},{24,0},{28,4},{1,25},{... | collective-permute-start | bytes 294920 | tf_op jit(solution)/shard_map/ppermute | solution.py:16
  6.1 1.5 %collective-permute-start.16 = (bf16[128,768]{1,0:T(8,128)(2,1)}, bf16[128,768]{1,0:T(8,128)(2,1)S(1)}, u32[]{:S(2)}, u32[]{:S(2)}) collective-permute-start(bf16[128,768]{1,0:T(8,128)(2,1)} %param.5), channel_id=1, source_target_pairs={{0,2},{1,3},{2,0},{3,1},{4,6},{5,7},{6,4},{7,5},{8,10},{9,11},{10,... | collective-permute-start | bytes 589832 | tf_op jit(solution)/shard_map/ppermute | solution.py:16
  7.6 1.5 %collective-permute-start.15 = (bf16[128,768]{1,0:T(8,128)(2,1)}, bf16[128,768]{1,0:T(8,128)(2,1)S(1)}, u32[]{:S(2)}, u32[]{:S(2)}) collective-permute-start(bf16[128,768]{1,0:T(8,128)(2,1)} %param.5), channel_id=1, source_target_pairs={{0,1},{1,0},{2,3},{3,2},{4,5},{5,4},{6,7},{7,6},{8,9},{9,8},{10,11... | collective-permute-start | bytes 589832 | tf_op jit(solution)/shard_map/ppermute | solution.py:16
  9.1 1.0 %constant_dynamic-update-slice_fusion.51 = bf16[512,768]{1,0:T(8,128)(2,1)S(1)} fusion(bf16[128,768]{1,0:T(8,128)(2,1)} %param.5), kind=kLoop, calls=%fused_computation.134 | loop fusion | bytes 393216
  10.1 0.9 %bitcast_dynamic-update-slice_fusion.7 = bf16[4,64,768]{2,1,0:T(8,128)(2,1)S(1)} fusion(bf16[4,64,768]{2,1,0:T(8,128)(2,1)S(1)} %broadcast.190.clone.1, s32[]{:T(128)S(6)} %select_n.177, bf16[64,768]{1,0:T(8,128)(2,1)} %param.6), kind=kLoop, calls=%fused_computation.127 | loop fusion | bytes 196612 | tf_op jit(solution)/shard_map/jit(dynamic_update_index_in_dim)/dynamic_update_slice | solution.py:61
  11.9 0.5 collective-permute-done.16
  12.4 1.2 %collective-permute-done.15 = bf16[128,768]{1,0:T(8,128)(2,1)S(1)} collective-permute-done((bf16[128,768]{1,0:T(8,128)(2,1)}, bf16[128,768]{1,0:T(8,128)(2,1)S(1)}, u32[]{:S(2)}, u32[]{:S(2)}) %collective-permute-start.15) | collective-permute-done | bytes 196640 | tf_op jit(solution)/shard_map/ppermute | solution.py:16
  13.7 0.6 collective-permute-start.17
  14.3 0.5 collective-permute-start.18
  14.8 0.5 collective-permute-start.23
  15.4 3.5 %collective-permute-done.18 = bf16[64,768]{1,0:T(8,128)(2,1)S(1)} collective-permute-done((bf16[64,768]{1,0:T(8,128)(2,1)S(1)}, bf16[64,768]{1,0:T(8,128)(2,1)S(1)}, u32[]{:S(2)}, u32[]{:S(2)}) %collective-permute-start.18) | collective-permute-done | bytes 98336 | tf_op jit(solution)/shard_map/ppermute | solution.py:16
  19.0 0.6 collective-permute-start.27
  19.7 1.3 %collective-permute-done.22 = bf16[64,768]{1,0:T(8,128)(2,1)S(1)} collective-permute-done((bf16[64,768]{1,0:T(8,128)(2,1)S(1)}, bf16[64,768]{1,0:T(8,128)(2,1)S(1)}, u32[]{:S(2)}, u32[]{:S(2)}) %collective-permute-start.22) | collective-permute-done | bytes 98336 | tf_op jit(solution)/shard_map/ppermute | solution.py:16
  21.1 0.4 collective-permute-start.29
  21.7 0.7 %collective-permute-done.28 = bf16[128,768]{1,0:T(8,128)(2,1)S(1)} collective-permute-done((bf16[128,768]{1,0:T(8,128)(2,1)S(1)}, bf16[128,768]{1,0:T(8,128)(2,1)S(1)}, u32[]{:S(2)}, u32[]{:S(2)}) %collective-permute-start.28) | collective-permute-done | bytes 196640 | tf_op jit(solution)/shard_map/ppermute | solution.py:16
  22.4 0.6 fusion.10
  23.1 0.6 fusion.11
  24.0 28.2 %collective-permute-start.30 = (f32[3,512]{1,0:T(4,128)S(1)}, f32[3,512]{1,0:T(4,128)S(1)}, u32[]{:S(2)}, u32[]{:S(2)}) collective-permute-start(f32[3,512]{1,0:T(4,128)S(1)} %get-tuple-element.98), channel_id=1, source_target_pairs={{0,4},{4,0},{8,12},{12,8},{16,20},{20,16},{24,28},{28,24},{1,5},{5... | collective-permute-start | bytes 18440 | tf_op jit(solution)/shard_map/ppermute | solution.py:16
  52.2 0.8 %collective-permute-done.30 = f32[3,512]{1,0:T(4,128)S(1)} collective-permute-done((f32[3,512]{1,0:T(4,128)S(1)}, f32[3,512]{1,0:T(4,128)S(1)}, u32[]{:S(2)}, u32[]{:S(2)}) %collective-permute-start.30) | collective-permute-done | bytes 6176 | tf_op jit(solution)/shard_map/ppermute | solution.py:16
  53.2 0.4 exponential_reduce_fusion.10
  53.6 0.4 fusion.16
  54.0 0.7 %copy-done.1 = bf16[512,768]{1,0:T(8,128)(2,1)S(1)} copy-done((bf16[512,768]{1,0:T(8,128)(2,1)S(1)}, bf16[512,768]{1,0:T(8,128)(2,1)}, u32[]{:S(2)}) %copy-start.1) | copy-done | bytes 786456
  54.7 0.4 convolution_add_fusion
  55.3 1.8 %collective-permute-start.31 = (bf16[72,768]{1,0:T(8,128)(2,1)S(1)}, bf16[72,768]{1,0:T(8,128)(2,1)S(1)}, u32[]{:S(2)}, u32[]{:S(2)}) collective-permute-start(bf16[72,768]{1,0:T(8,128)(2,1)S(1)} %get-tuple-element.88), channel_id=1, source_target_pairs={{0,8},{4,12},{8,0},{12,4},{16,24},{20,28},{24,16},{28,20},{1,9},{5... | collective-permute-start | bytes 331784 | tf_op jit(solution)/shard_map/ppermute | solution.py:16
  57.3 1.2 %collective-permute-start.32 = (bf16[72,768]{1,0:T(8,128)(2,1)S(1)}, bf16[72,768]{1,0:T(8,128)(2,1)S(1)}, u32[]{:S(2)}, u32[]{:S(2)}) collective-permute-start(bf16[72,768]{1,0:T(8,128)(2,1)S(1)} %get-tuple-element.89), channel_id=1, source_target_pairs={{0,16},{4,20},{8,24},{12,28},{16,0},{20,4},{24,8},{28,12},{1,17},{... | collective-permute-start | bytes 331784 | tf_op jit(solution)/shard_map/ppermute | solution.py:16
  58.5 1.5 %collective-permute-start.33 = (bf16[72,768]{1,0:T(8,128)(2,1)S(1)}, bf16[72,768]{1,0:T(8,128)(2,1)S(1)}, u32[]{:S(2)}, u32[]{:S(2)}) collective-permute-start(bf16[72,768]{1,0:T(8,128)(2,1)S(1)} %get-tuple-element.90), channel_id=1, source_target_pairs={{0,24},{4,28},{8,16},{12,20},{16,8},{20,12},{24,0},{28,4},{1,25},{... | collective-permute-start | bytes 331784 | tf_op jit(solution)/shard_map/ppermute | solution.py:16
  60.0 0.7 collective-permute-done.31
  60.8 7.8 %collective-permute-done.32 = bf16[72,768]{1,0:T(8,128)(2,1)S(1)} collective-permute-done((bf16[72,768]{1,0:T(8,128)(2,1)S(1)}, bf16[72,768]{1,0:T(8,128)(2,1)S(1)}, u32[]{:S(2)}, u32[]{:S(2)}) %collective-permute-start.32) | collective-permute-done | bytes 110624 | tf_op jit(solution)/shard_map/ppermute | solution.py:16
  68.6 0.6 copy.15
  69.4 0.7 reshape.504
  70.1 0.7 %fusion.24 = bf16[64,768]{1,0:T(8,128)(2,1)} fusion(f32[1,4,64,768]{3,2,1,0:T(8,128)S(1)} %bitcast.71, s32[]{:T(128)S(6)} %select_n.177, bf16[72,768]{1,0:T(8,128)(2,1)S(1)} %collective-permute-done.33, bf16[72,768]{1,0:T(8,128)(2,1)S(1)} %collective-permute-done.32, bf16[72,768]{1,0:T(8,128)(2,1)S(1)} %collective-permute-done.31, f32[64]{0:T(128)S(1)} %fusion.58), kind=kLoop, calls=%fused_computation.115 | loop fusion | flops 393216 | bytes 590084 | tf_op jit(solution)/shard_map/convert_element_type | solution.py:230
  (90 shorter events, 2.6 us)
Async XLA Ops:
  0.6 10.4 %copy-start.4 = (s32[4,4]{1,0:T(4,128)S(1)}, s32[4,4]{1,0:T(4,128)}, u32[]{:S(2)}) copy-start(s32[4,4]{1,0:T(4,128)} %param.7) | copy-start | bytes 196
  0.6 14.1 %collective-permute-start.19 = (bf16[64,768]{1,0:T(8,128)(2,1)}, bf16[64,768]{1,0:T(8,128)(2,1)S(1)}, u32[]{:S(2)}, u32[]{:S(2)}) collective-permute-start(bf16[64,768]{1,0:T(8,128)(2,1)} %param.6), channel_id=1, source_target_pairs={{0,16},{4,20},{8,24},{12,28},{16,0},{20,4},{24,8},{28,12},{1,17},{... | collective-permute-start | bytes 294920 | tf_op jit(solution)/shard_map/ppermute | solution.py:16
  4.7 10.0 %collective-permute-start.20 = (bf16[64,768]{1,0:T(8,128)(2,1)}, bf16[64,768]{1,0:T(8,128)(2,1)S(1)}, u32[]{:S(2)}, u32[]{:S(2)}) collective-permute-start(bf16[64,768]{1,0:T(8,128)(2,1)} %param.6), channel_id=1, source_target_pairs={{0,24},{4,28},{8,16},{12,20},{16,8},{20,12},{24,0},{28,4},{1,25},{... | collective-permute-start | bytes 294920 | tf_op jit(solution)/shard_map/ppermute | solution.py:16
  6.1 6.3 %collective-permute-start.16 = (bf16[128,768]{1,0:T(8,128)(2,1)}, bf16[128,768]{1,0:T(8,128)(2,1)S(1)}, u32[]{:S(2)}, u32[]{:S(2)}) collective-permute-start(bf16[128,768]{1,0:T(8,128)(2,1)} %param.5), channel_id=1, source_target_pairs={{0,2},{1,3},{2,0},{3,1},{4,6},{5,7},{6,4},{7,5},{8,10},{9,11},{10,... | collective-permute-start | bytes 589832 | tf_op jit(solution)/shard_map/ppermute | solution.py:16
  7.6 6.0 %collective-permute-start.15 = (bf16[128,768]{1,0:T(8,128)(2,1)}, bf16[128,768]{1,0:T(8,128)(2,1)S(1)}, u32[]{:S(2)}, u32[]{:S(2)}) collective-permute-start(bf16[128,768]{1,0:T(8,128)(2,1)} %param.5), channel_id=1, source_target_pairs={{0,1},{1,0},{2,3},{3,2},{4,5},{5,4},{6,7},{7,6},{8,9},{9,8},{10,11... | collective-permute-start | bytes 589832 | tf_op jit(solution)/shard_map/ppermute | solution.py:16
  9.1 2.0 %collective-permute-start.25 = (s32[4,4]{1,0:T(4,128)}, s32[4,4]{1,0:T(4,128)S(1)}, u32[]{:S(2)}, u32[]{:S(2)}) collective-permute-start(s32[4,4]{1,0:T(4,128)} %param.7), channel_id=1, source_target_pairs={{0,4},{4,0},{8,12},{12,8},{16,20},{20,16},{24,28},{28,24},{1,5},{5... | collective-permute-start | bytes 200 | tf_op jit(solution)/shard_map/ppermute | solution.py:16
  11.6 2.7 %copy-start.3 = (bf16[64,768]{1,0:T(8,128)(2,1)S(1)}, bf16[64,768]{1,0:T(8,128)(2,1)}, u32[]{:S(2)}) copy-start(bf16[64,768]{1,0:T(8,128)(2,1)} %param.6) | copy-start | bytes 294916
  11.9 7.0 %copy-start.2 = (bf16[128,768]{1,0:T(8,128)(2,1)S(1)}, bf16[128,768]{1,0:T(8,128)(2,1)}, u32[]{:S(2)}) copy-start(bf16[128,768]{1,0:T(8,128)(2,1)} %param.5) | copy-start | bytes 589828
  13.7 5.9 %collective-permute-start.17 = (bf16[128,768]{1,0:T(8,128)(2,1)S(1)}, bf16[128,768]{1,0:T(8,128)(2,1)S(1)}, u32[]{:S(2)}, u32[]{:S(2)}) collective-permute-start(bf16[128,768]{1,0:T(8,128)(2,1)S(1)} %get-tuple-element.79), channel_id=1, source_target_pairs={{0,2},{1,3},{2,0},{3,1},{4,5},{5,4},{6,7},{7,6},{8,10},{9,11},{10,... | collective-permute-start | bytes 589832 | tf_op jit(solution)/shard_map/ppermute | solution.py:23
  14.3 4.6 %collective-permute-start.18 = (bf16[64,768]{1,0:T(8,128)(2,1)S(1)}, bf16[64,768]{1,0:T(8,128)(2,1)S(1)}, u32[]{:S(2)}, u32[]{:S(2)}) collective-permute-start(bf16[64,768]{1,0:T(8,128)(2,1)S(1)} %copy-done.3), channel_id=1, source_target_pairs={{0,8},{4,12},{8,0},{12,4},{16,24},{20,28},{24,16},{28,20},{1,9},{5... | collective-permute-start | bytes 294920 | tf_op jit(solution)/shard_map/ppermute | solution.py:16
  14.8 4.2 %collective-permute-start.21 = (bf16[64,768]{1,0:T(8,128)(2,1)S(1)}, bf16[64,768]{1,0:T(8,128)(2,1)S(1)}, u32[]{:S(2)}, u32[]{:S(2)}) collective-permute-start(bf16[64,768]{1,0:T(8,128)(2,1)S(1)} %copy-done.3), channel_id=1, source_target_pairs={{0,4},{4,0},{8,12},{12,8},{16,20},{20,16},{24,28},{28,24},{1,5},{5... | collective-permute-start | bytes 294920 | tf_op jit(solution)/shard_map/ppermute | solution.py:16
  14.8 6.8 %collective-permute-start.23 = (bf16[64,768]{1,0:T(8,128)(2,1)S(1)}, bf16[64,768]{1,0:T(8,128)(2,1)S(1)}, u32[]{:S(2)}, u32[]{:S(2)}) collective-permute-start(bf16[64,768]{1,0:T(8,128)(2,1)S(1)} %collective-permute-done.19), channel_id=1, source_target_pairs={{0,4},{4,0},{8,12},{12,8},{16,20},{20,16},{24,28},{28,24},{1,5},{5... | collective-permute-start | bytes 294920 | tf_op jit(solution)/shard_map/ppermute | solution.py:16
  15.3 6.4 %collective-permute-start.24 = (bf16[64,768]{1,0:T(8,128)(2,1)S(1)}, bf16[64,768]{1,0:T(8,128)(2,1)S(1)}, u32[]{:S(2)}, u32[]{:S(2)}) collective-permute-start(bf16[64,768]{1,0:T(8,128)(2,1)S(1)} %collective-permute-done.20), channel_id=1, source_target_pairs={{0,4},{4,0},{8,12},{12,8},{16,20},{20,16},{24,28},{28,24},{1,5},{5... | collective-permute-start | bytes 294920 | tf_op jit(solution)/shard_map/ppermute | solution.py:16
  18.9 2.2 %collective-permute-start.26 = (bf16[128,768]{1,0:T(8,128)(2,1)S(1)}, bf16[128,768]{1,0:T(8,128)(2,1)S(1)}, u32[]{:S(2)}, u32[]{:S(2)}) collective-permute-start(bf16[128,768]{1,0:T(8,128)(2,1)S(1)} %copy-done.2), channel_id=1, source_target_pairs={{0,4},{4,0},{8,12},{12,8},{16,20},{20,16},{24,28},{28,24},{1,5},{5... | collective-permute-start | bytes 589832 | tf_op jit(solution)/shard_map/ppermute | solution.py:16
  19.0 2.7 %collective-permute-start.27 = (bf16[128,768]{1,0:T(8,128)(2,1)S(1)}, bf16[128,768]{1,0:T(8,128)(2,1)S(1)}, u32[]{:S(2)}, u32[]{:S(2)}) collective-permute-start(bf16[128,768]{1,0:T(8,128)(2,1)S(1)} %collective-permute-done.15), channel_id=1, source_target_pairs={{0,4},{4,0},{8,12},{12,8},{16,20},{20,16},{24,28},{28,24},{1,5},{5... | collective-permute-start | bytes 589832 | tf_op jit(solution)/shard_map/ppermute | solution.py:16
  19.6 1.4 %collective-permute-start.22 = (bf16[64,768]{1,0:T(8,128)(2,1)S(1)}, bf16[64,768]{1,0:T(8,128)(2,1)S(1)}, u32[]{:S(2)}, u32[]{:S(2)}) collective-permute-start(bf16[64,768]{1,0:T(8,128)(2,1)S(1)} %collective-permute-done.18), channel_id=1, source_target_pairs={{0,4},{4,0},{8,12},{12,8},{16,20},{20,16},{24,28},{28,24},{1,5},{5... | collective-permute-start | bytes 294920 | tf_op jit(solution)/shard_map/ppermute | solution.py:16
  21.0 1.4 %collective-permute-start.28 = (bf16[128,768]{1,0:T(8,128)(2,1)S(1)}, bf16[128,768]{1,0:T(8,128)(2,1)S(1)}, u32[]{:S(2)}, u32[]{:S(2)}) collective-permute-start(bf16[128,768]{1,0:T(8,128)(2,1)S(1)} %collective-permute-done.16), channel_id=1, source_target_pairs={{0,4},{4,0},{8,12},{12,8},{16,20},{20,16},{24,28},{28,24},{1,5},{5... | collective-permute-start | bytes 589832 | tf_op jit(solution)/shard_map/ppermute | solution.py:16
  21.1 1.9 %collective-permute-start.29 = (bf16[128,768]{1,0:T(8,128)(2,1)S(1)}, bf16[128,768]{1,0:T(8,128)(2,1)S(1)}, u32[]{:S(2)}, u32[]{:S(2)}) collective-permute-start(bf16[128,768]{1,0:T(8,128)(2,1)S(1)} %collective-permute-done.17), channel_id=1, source_target_pairs={{0,4},{4,0},{8,12},{12,8},{16,20},{20,16},{24,28},{28,24},{1,5},{5... | collective-permute-start | bytes 589832 | tf_op jit(solution)/shard_map/ppermute | solution.py:16
  23.1 0.9 %copy-start = (bf16[512,768]{1,0:T(8,128)(2,1)}, bf16[512,768]{1,0:T(8,128)(2,1)S(1)}, u32[]{:S(2)}) copy-start(bf16[512,768]{1,0:T(8,128)(2,1)S(1)} %constant_dynamic-update-slice_fusion.52) | copy-start | bytes 2359300
  24.0 29.1 %collective-permute-start.30 = (f32[3,512]{1,0:T(4,128)S(1)}, f32[3,512]{1,0:T(4,128)S(1)}, u32[]{:S(2)}, u32[]{:S(2)}) collective-permute-start(f32[3,512]{1,0:T(4,128)S(1)} %get-tuple-element.98), channel_id=1, source_target_pairs={{0,4},{4,0},{8,12},{12,8},{16,20},{20,16},{24,28},{28,24},{1,5},{5... | collective-permute-start | bytes 18440 | tf_op jit(solution)/shard_map/ppermute | solution.py:16
  53.6 1.1 %copy-start.1 = (bf16[512,768]{1,0:T(8,128)(2,1)S(1)}, bf16[512,768]{1,0:T(8,128)(2,1)}, u32[]{:S(2)}) copy-start(bf16[512,768]{1,0:T(8,128)(2,1)} %copy-done) | copy-start | bytes 2359300
  55.3 5.4 %collective-permute-start.31 = (bf16[72,768]{1,0:T(8,128)(2,1)S(1)}, bf16[72,768]{1,0:T(8,128)(2,1)S(1)}, u32[]{:S(2)}, u32[]{:S(2)}) collective-permute-start(bf16[72,768]{1,0:T(8,128)(2,1)S(1)} %get-tuple-element.88), channel_id=1, source_target_pairs={{0,8},{4,12},{8,0},{12,4},{16,24},{20,28},{24,16},{28,20},{1,9},{5... | collective-permute-start | bytes 331784 | tf_op jit(solution)/shard_map/ppermute | solution.py:16
  57.3 11.3 %collective-permute-start.32 = (bf16[72,768]{1,0:T(8,128)(2,1)S(1)}, bf16[72,768]{1,0:T(8,128)(2,1)S(1)}, u32[]{:S(2)}, u32[]{:S(2)}) collective-permute-start(bf16[72,768]{1,0:T(8,128)(2,1)S(1)} %get-tuple-element.89), channel_id=1, source_target_pairs={{0,16},{4,20},{8,24},{12,28},{16,0},{20,4},{24,8},{28,12},{1,17},{... | collective-permute-start | bytes 331784 | tf_op jit(solution)/shard_map/ppermute | solution.py:16
  58.5 10.7 %collective-permute-start.33 = (bf16[72,768]{1,0:T(8,128)(2,1)S(1)}, bf16[72,768]{1,0:T(8,128)(2,1)S(1)}, u32[]{:S(2)}, u32[]{:S(2)}) collective-permute-start(bf16[72,768]{1,0:T(8,128)(2,1)S(1)} %get-tuple-element.90), channel_id=1, source_target_pairs={{0,24},{4,28},{8,16},{12,20},{16,8},{20,12},{24,0},{28,4},{1,25},{... | collective-permute-start | bytes 331784 | tf_op jit(solution)/shard_map/ppermute | solution.py:16
where the time goes:
time: 71.1 us; the launch traced here: 70.9 us
  starting transfers between devices  44 us (62%)
  waiting for transfers between devices  16.6 us (23%)
  local copies, waits for them, and re-layouts  5 us (7%)
  matrix products  2.56 us (4%)
  other arithmetic  1.65 us (2%)
  between operations  1.06 us (1%)
    ppermute x18, starting transfers between devices, swap(): lax.ppermute(x, axis, [(i, i ^ k) for i in range(lax.axis_size(axis))])  43.5 us
    ppermute x18, waiting for transfers between devices, swap(): lax.ppermute(x, axis, [(i, i ^ k) for i in range(lax.axis_size(axis))])  16.6 us
    unnamed x18, local copies, waits for them, and re-layouts  2.6 us
  transfers between devices with their start and end apart: 19, of which 8 were waited for; matrix products, arithmetic and copies ran while one was open for 6% of the time, Pallas kernels for 0%

commit v1 on v0

--- a/solution.py
+++ b/solution.py
@@ -62,10 +62,10 @@
     return whole.reshape((-1,) + parts[0].shape[1:])
 
 
-def gather_centroids(x, first, ready):
+def gather_centroids(x, ready):
     for at, size in stages("row"):
-        parts = [x] + [swap(after(x, first) if d << at == 2 else x, "row", d << at) for d in range(1, size)]
-        mate = [swap(after(part, ready), "row", 1) for part in parts]
+        parts = [x] + [after(swap(x, "row", d << at), ready) for d in range(1, size)]
+        mate = [swap(after(part, ready) if part is x else part, "row", 1) for part in parts]
         position = digit("row", at, size)
         x = placed(parts, position)
     return jnp.concatenate([x, placed(mate, position)])
@@ -84,6 +84,14 @@
         x = jnp.where((index & bit) != 0, pairs[:, ::-1], pairs).reshape(shape)
         bit *= 2
     return x
+
+
+def unxor_list(parts, index):
+    bit = 1
+    while bit < len(parts):
+        parts = [jnp.where((index & bit) != 0, parts[p ^ bit], part) for p, part in enumerate(parts)]
+        bit *= 2
+    return parts
 
 
 def tree(op, parts):
@@ -144,9 +152,9 @@
     mass_ratio = group_cols * cols / (row_count * rows)
     target = 1 / mass_ratio
 
-    mate_pattern = swap(pattern, "row", 1)
     own_parts, mate_parts, first, ready = gather_spans(spans, core)
-    tile_centroids = gather_centroids(centroids, first, ready)
+    mate_pattern = swap(after(pattern, first), "row", 1)
+    tile_centroids = gather_centroids(centroids, ready)
     span_halves = [jnp.concatenate(own_parts), jnp.concatenate(mate_parts)]
     at = jnp.arange(group_cols)
     row_of = at % half_cols // per * 2 + (at // half_cols ^ core)
@@ -219,7 +227,8 @@
             block = lax.dynamic_index_in_dim(low, me ^ d, 1, keepdims=False).reshape(-1, width)
             got = swap(jnp.concatenate([block, note]), "row", d << at)
             if d << at == 2:
-                row_out = unxor(after(row_pot[:row_count], got), me_col, cols)
+                row_out = after(row_pot[:row_count], got)
+                row_out = jnp.concatenate(unxor_list(jnp.split(row_out, cols), me_col))
             parts.append(got[: block.shape[0]].astype(jnp.float32).reshape(parts[0].shape))
             masses.append(from_thirds(got[block.shape[0] :], group_cols))
         held, mass = add(parts), add(masses)

time: 71.1 us -> 70.4 us (level)
  waiting for transfers between devices: 16.6 us -> 14.1 us
  starting transfers between devices: 44 us -> 45.5 us
    ppermute x18, waiting for transfers between devices: 16.6 us -> 12.9 us  [swap(): lax.ppermute(x, axis, [(i, i ^ k) for i in range(lax.axis_size(axis))])]
    ppermute x18, starting transfers between devices: 43.5 us -> 45 us  [swap(): lax.ppermute(x, axis, [(i, i ^ k) for i in range(lax.axis_size(axis))])]
    ppermute x1, waiting for transfers between devices: 0.01 us -> 1.22 us  [swap_by_core(): return lax.ppermute(x, ('row', 'col'), pairs)]
    unnamed x18 -> x17, local copies, waits for them, and re-layouts: 2.6 us -> 2.28 us
where the time goes in v1:
time: 70.4 us; the launch traced here: 70.1 us
  starting transfers between devices  45.5 us (65%)
  waiting for transfers between devices  14.1 us (20%)
  local copies, waits for them, and re-layouts  4.6 us (7%)
  matrix products  2.56 us (4%)
  other arithmetic  2.23 us (3%)
  between operations  1.08 us (2%)
    ppermute x18, starting transfers between devices, swap(): lax.ppermute(x, axis, [(i, i ^ k) for i in range(lax.axis_size(axis))])  45 us
    ppermute x18, waiting for transfers between devices, swap(): lax.ppermute(x, axis, [(i, i ^ k) for i in range(lax.axis_size(axis))])  12.9 us
    unnamed x17, local copies, waits for them, and re-layouts  2.28 us
  transfers between devices with their start and end apart: 19, of which 8 were waited for; matrix products, arithmetic and copies ran while one was open for 6% of the time, Pallas kernels for 0%

profile of v1, /device:TPU:0, one launch (start us, length us, event | category | flops | bytes accessed | tf_op | source)
XLA Modules:
  0.0 70.1 jit_solution(12915706694790593541)
XLA Ops:
  0.6 4.1 %collective-permute-start.19 = (bf16[64,768]{1,0:T(8,128)(2,1)}, bf16[64,768]{1,0:T(8,128)(2,1)S(1)}, u32[]{:S(2)}, u32[]{:S(2)}) collective-permute-start(bf16[64,768]{1,0:T(8,128)(2,1)} %param.6), channel_id=1, source_target_pairs={{0,16},{4,20},{8,24},{12,28},{16,0},{20,4},{24,8},{28,12},{1,17},{... | collective-permute-start | bytes 294920 | tf_op jit(solution)/shard_map/ppermute | solution.py:16
  4.7 1.6 %collective-permute-start.18 = (bf16[64,768]{1,0:T(8,128)(2,1)}, bf16[64,768]{1,0:T(8,128)(2,1)S(1)}, u32[]{:S(2)}, u32[]{:S(2)}) collective-permute-start(bf16[64,768]{1,0:T(8,128)(2,1)} %param.6), channel_id=1, source_target_pairs={{0,8},{4,12},{8,0},{12,4},{16,24},{20,28},{24,16},{28,20},{1,9},{5... | collective-permute-start | bytes 294920 | tf_op jit(solution)/shard_map/ppermute | solution.py:16
  6.3 1.7 %collective-permute-start.16 = (bf16[128,768]{1,0:T(8,128)(2,1)}, bf16[128,768]{1,0:T(8,128)(2,1)S(1)}, u32[]{:S(2)}, u32[]{:S(2)}) collective-permute-start(bf16[128,768]{1,0:T(8,128)(2,1)} %param.5), channel_id=1, source_target_pairs={{0,2},{1,3},{2,0},{3,1},{4,6},{5,7},{6,4},{7,5},{8,10},{9,11},{10,... | collective-permute-start | bytes 589832 | tf_op jit(solution)/shard_map/ppermute | solution.py:16
  8.1 1.5 %collective-permute-start.15 = (bf16[128,768]{1,0:T(8,128)(2,1)}, bf16[128,768]{1,0:T(8,128)(2,1)S(1)}, u32[]{:S(2)}, u32[]{:S(2)}) collective-permute-start(bf16[128,768]{1,0:T(8,128)(2,1)} %param.5), channel_id=1, source_target_pairs={{0,1},{1,0},{2,3},{3,2},{4,5},{5,4},{6,7},{7,6},{8,9},{9,8},{10,11... | collective-permute-start | bytes 589832 | tf_op jit(solution)/shard_map/ppermute | solution.py:16
  9.6 1.0 %constant_dynamic-update-slice_fusion.51 = bf16[512,768]{1,0:T(8,128)(2,1)S(1)} fusion(bf16[128,768]{1,0:T(8,128)(2,1)} %param.5), kind=kLoop, calls=%fused_computation.134 | loop fusion | bytes 393216
  10.6 1.0 %bitcast_dynamic-update-slice_fusion.7 = bf16[4,64,768]{2,1,0:T(8,128)(2,1)S(1)} fusion(bf16[4,64,768]{2,1,0:T(8,128)(2,1)S(1)} %broadcast.190.clone.1, s32[]{:T(128)S(6)} %select_n.199, bf16[64,768]{1,0:T(8,128)(2,1)} %param.6), kind=kLoop, calls=%fused_computation.127 | loop fusion | bytes 196612 | tf_op jit(solution)/shard_map/jit(dynamic_update_index_in_dim)/dynamic_update_slice | solution.py:61
  11.6 1.0 %collective-permute-done.16 = bf16[128,768]{1,0:T(8,128)(2,1)S(1)} collective-permute-done((bf16[128,768]{1,0:T(8,128)(2,1)}, bf16[128,768]{1,0:T(8,128)(2,1)S(1)}, u32[]{:S(2)}, u32[]{:S(2)}) %collective-permute-start.16) | collective-permute-done | bytes 196640 | tf_op jit(solution)/shard_map/ppermute | solution.py:16
  12.6 1.3 %collective-permute-done.15 = bf16[128,768]{1,0:T(8,128)(2,1)S(1)} collective-permute-done((bf16[128,768]{1,0:T(8,128)(2,1)}, bf16[128,768]{1,0:T(8,128)(2,1)S(1)}, u32[]{:S(2)}, u32[]{:S(2)}) %collective-permute-start.15) | collective-permute-done | bytes 196640 | tf_op jit(solution)/shard_map/ppermute | solution.py:16
  14.0 0.5 collective-permute-start.17
  14.5 0.6 collective-permute-start.22
  15.1 0.4 collective-permute-start.24
  16.7 0.4 collective-permute-done.21
  17.3 0.4 collective-permute-start.26
  18.0 0.5 collective-permute-start.28
  18.5 1.2 %collective-permute-done.17 = bf16[128,768]{1,0:T(8,128)(2,1)S(1)} collective-permute-done((bf16[128,768]{1,0:T(8,128)(2,1)S(1)}, bf16[128,768]{1,0:T(8,128)(2,1)S(1)}, u32[]{:S(2)}, u32[]{:S(2)}) %collective-permute-start.17) | collective-permute-done | bytes 196640 | tf_op jit(solution)/shard_map/ppermute | solution.py:23
  19.9 0.6 fusion.10
  20.5 0.7 %collective-permute-done.29 = bf16[128,768]{1,0:T(8,128)(2,1)S(1)} collective-permute-done((bf16[128,768]{1,0:T(8,128)(2,1)S(1)}, bf16[128,768]{1,0:T(8,128)(2,1)S(1)}, u32[]{:S(2)}, u32[]{:S(2)}) %collective-permute-start.29) | collective-permute-done | bytes 196640 | tf_op jit(solution)/shard_map/ppermute | solution.py:16
  21.2 0.6 fusion.11
  22.1 29.4 %collective-permute-start.30 = (f32[3,512]{1,0:T(4,128)S(1)}, f32[3,512]{1,0:T(4,128)S(1)}, u32[]{:S(2)}, u32[]{:S(2)}) collective-permute-start(f32[3,512]{1,0:T(4,128)S(1)} %get-tuple-element.102), channel_id=1, source_target_pairs={{0,4},{4,0},{8,12},{12,8},{16,20},{20,16},{24,28},{28,24},{1,5},{5... | collective-permute-start | bytes 18440 | tf_op jit(solution)/shard_map/ppermute | solution.py:16
  51.5 0.8 %collective-permute-done.30 = f32[3,512]{1,0:T(4,128)S(1)} collective-permute-done((f32[3,512]{1,0:T(4,128)S(1)}, f32[3,512]{1,0:T(4,128)S(1)}, u32[]{:S(2)}, u32[]{:S(2)}) %collective-permute-start.30) | collective-permute-done | bytes 6176 | tf_op jit(solution)/shard_map/ppermute | solution.py:16
  52.4 0.4 exponential_reduce_fusion.10
  52.9 0.4 fusion.16
  53.3 0.7 %copy-done.1 = bf16[512,768]{1,0:T(8,128)(2,1)S(1)} copy-done((bf16[512,768]{1,0:T(8,128)(2,1)S(1)}, bf16[512,768]{1,0:T(8,128)(2,1)}, u32[]{:S(2)}) %copy-start.1) | copy-done | bytes 786456
  54.0 0.4 convolution_add_fusion
  54.5 1.8 %collective-permute-start.31 = (bf16[72,768]{1,0:T(8,128)(2,1)S(1)}, bf16[72,768]{1,0:T(8,128)(2,1)S(1)}, u32[]{:S(2)}, u32[]{:S(2)}) collective-permute-start(bf16[72,768]{1,0:T(8,128)(2,1)S(1)} %get-tuple-element.88), channel_id=1, source_target_pairs={{0,8},{4,12},{8,0},{12,4},{16,24},{20,28},{24,16},{28,20},{1,9},{5... | collective-permute-start | bytes 331784 | tf_op jit(solution)/shard_map/ppermute | solution.py:16
  56.6 1.2 %collective-permute-start.32 = (bf16[72,768]{1,0:T(8,128)(2,1)S(1)}, bf16[72,768]{1,0:T(8,128)(2,1)S(1)}, u32[]{:S(2)}, u32[]{:S(2)}) collective-permute-start(bf16[72,768]{1,0:T(8,128)(2,1)S(1)} %get-tuple-element.89), channel_id=1, source_target_pairs={{0,16},{4,20},{8,24},{12,28},{16,0},{20,4},{24,8},{28,12},{1,17},{... | collective-permute-start | bytes 331784 | tf_op jit(solution)/shard_map/ppermute | solution.py:16
  57.8 1.5 %collective-permute-start.33 = (bf16[72,768]{1,0:T(8,128)(2,1)S(1)}, bf16[72,768]{1,0:T(8,128)(2,1)S(1)}, u32[]{:S(2)}, u32[]{:S(2)}) collective-permute-start(bf16[72,768]{1,0:T(8,128)(2,1)S(1)} %get-tuple-element.90), channel_id=1, source_target_pairs={{0,24},{4,28},{8,16},{12,20},{16,8},{20,12},{24,0},{28,4},{1,25},{... | collective-permute-start | bytes 331784 | tf_op jit(solution)/shard_map/ppermute | solution.py:16
  59.2 0.7 collective-permute-done.31
  59.9 7.9 %collective-permute-done.32 = bf16[72,768]{1,0:T(8,128)(2,1)S(1)} collective-permute-done((bf16[72,768]{1,0:T(8,128)(2,1)S(1)}, bf16[72,768]{1,0:T(8,128)(2,1)S(1)}, u32[]{:S(2)}, u32[]{:S(2)}) %collective-permute-start.32) | collective-permute-done | bytes 110624 | tf_op jit(solution)/shard_map/ppermute | solution.py:16
  68.1 0.7 reshape.496
  68.8 0.6 pad_maximum_fusion.9
  69.4 0.7 %fusion.24 = bf16[64,768]{1,0:T(8,128)(2,1)} fusion(f32[1,4,64,768]{3,2,1,0:T(8,128)S(1)} %bitcast.67, s32[]{:T(128)S(6)} %select_n.199, bf16[72,768]{1,0:T(8,128)(2,1)S(1)} %collective-permute-done.33, bf16[72,768]{1,0:T(8,128)(2,1)S(1)} %collective-permute-done.32, bf16[72,768]{1,0:T(8,128)(2,1)S(1)} %collective-permute-done.31, f32[64]{0:T(128)S(1)} %fusion.58), kind=kLoop, calls=%fused_computation.115 | loop fusion | flops 393216 | bytes 590084 | tf_op jit(solution)/shard_map/convert_element_type | solution.py:239
  (86 shorter events, 2.7 us)
Async XLA Ops:
  0.6 13.8 %copy-start.4 = (s32[4,4]{1,0:T(4,128)S(1)}, s32[4,4]{1,0:T(4,128)}, u32[]{:S(2)}) copy-start(s32[4,4]{1,0:T(4,128)} %param.7) | copy-start | bytes 196
  0.6 13.9 %collective-permute-start.19 = (bf16[64,768]{1,0:T(8,128)(2,1)}, bf16[64,768]{1,0:T(8,128)(2,1)S(1)}, u32[]{:S(2)}, u32[]{:S(2)}) collective-permute-start(bf16[64,768]{1,0:T(8,128)(2,1)} %param.6), channel_id=1, source_target_pairs={{0,16},{4,20},{8,24},{12,28},{16,0},{20,4},{24,8},{28,12},{1,17},{... | collective-permute-start | bytes 294920 | tf_op jit(solution)/shard_map/ppermute | solution.py:16
  4.7 9.8 %collective-permute-start.18 = (bf16[64,768]{1,0:T(8,128)(2,1)}, bf16[64,768]{1,0:T(8,128)(2,1)S(1)}, u32[]{:S(2)}, u32[]{:S(2)}) collective-permute-start(bf16[64,768]{1,0:T(8,128)(2,1)} %param.6), channel_id=1, source_target_pairs={{0,8},{4,12},{8,0},{12,4},{16,24},{20,28},{24,16},{28,20},{1,9},{5... | collective-permute-start | bytes 294920 | tf_op jit(solution)/shard_map/ppermute | solution.py:16
  6.3 8.2 %collective-permute-start.20 = (bf16[64,768]{1,0:T(8,128)(2,1)}, bf16[64,768]{1,0:T(8,128)(2,1)S(1)}, u32[]{:S(2)}, u32[]{:S(2)}) collective-permute-start(bf16[64,768]{1,0:T(8,128)(2,1)} %param.6), channel_id=1, source_target_pairs={{0,24},{4,28},{8,16},{12,20},{16,8},{20,12},{24,0},{28,4},{1,25},{... | collective-permute-start | bytes 294920 | tf_op jit(solution)/shard_map/ppermute | solution.py:16
  6.3 6.3 %collective-permute-start.16 = (bf16[128,768]{1,0:T(8,128)(2,1)}, bf16[128,768]{1,0:T(8,128)(2,1)S(1)}, u32[]{:S(2)}, u32[]{:S(2)}) collective-permute-start(bf16[128,768]{1,0:T(8,128)(2,1)} %param.5), channel_id=1, source_target_pairs={{0,2},{1,3},{2,0},{3,1},{4,6},{5,7},{6,4},{7,5},{8,10},{9,11},{10,... | collective-permute-start | bytes 589832 | tf_op jit(solution)/shard_map/ppermute | solution.py:16
  8.1 5.9 %collective-permute-start.15 = (bf16[128,768]{1,0:T(8,128)(2,1)}, bf16[128,768]{1,0:T(8,128)(2,1)S(1)}, u32[]{:S(2)}, u32[]{:S(2)}) collective-permute-start(bf16[128,768]{1,0:T(8,128)(2,1)} %param.5), channel_id=1, source_target_pairs={{0,1},{1,0},{2,3},{3,2},{4,5},{5,4},{6,7},{7,6},{8,9},{9,8},{10,11... | collective-permute-start | bytes 589832 | tf_op jit(solution)/shard_map/ppermute | solution.py:16
  10.6 5.1 %copy-start.3 = (bf16[64,768]{1,0:T(8,128)(2,1)S(1)}, bf16[64,768]{1,0:T(8,128)(2,1)}, u32[]{:S(2)}) copy-start(bf16[64,768]{1,0:T(8,128)(2,1)} %param.6) | copy-start | bytes 294916
  14.0 5.7 %collective-permute-start.17 = (bf16[128,768]{1,0:T(8,128)(2,1)S(1)}, bf16[128,768]{1,0:T(8,128)(2,1)S(1)}, u32[]{:S(2)}, u32[]{:S(2)}) collective-permute-start(bf16[128,768]{1,0:T(8,128)(2,1)S(1)} %get-tuple-element.79), channel_id=1, source_target_pairs={{0,2},{1,3},{2,0},{3,1},{4,5},{5,4},{6,7},{7,6},{8,10},{9,11},{10,... | collective-permute-start | bytes 589832 | tf_op jit(solution)/shard_map/ppermute | solution.py:23
  14.5 1.2 %collective-permute-start.25 = (s32[4,4]{1,0:T(4,128)S(1)}, s32[4,4]{1,0:T(4,128)S(1)}, u32[]{:S(2)}, u32[]{:S(2)}) collective-permute-start(s32[4,4]{1,0:T(4,128)S(1)} %copy-done.4), channel_id=1, source_target_pairs={{0,4},{4,0},{8,12},{12,8},{16,20},{20,16},{24,28},{28,24},{1,5},{5... | collective-permute-start | bytes 200 | tf_op jit(solution)/shard_map/ppermute | solution.py:16
  14.5 3.3 %collective-permute-start.22 = (bf16[64,768]{1,0:T(8,128)(2,1)S(1)}, bf16[64,768]{1,0:T(8,128)(2,1)S(1)}, u32[]{:S(2)}, u32[]{:S(2)}) collective-permute-start(bf16[64,768]{1,0:T(8,128)(2,1)S(1)} %collective-permute-done.18), channel_id=1, source_target_pairs={{0,4},{4,0},{8,12},{12,8},{16,20},{20,16},{24,28},{28,24},{1,5},{5... | collective-permute-start | bytes 294920 | tf_op jit(solution)/shard_map/ppermute | solution.py:16
  15.1 2.9 %collective-permute-start.23 = (bf16[64,768]{1,0:T(8,128)(2,1)S(1)}, bf16[64,768]{1,0:T(8,128)(2,1)S(1)}, u32[]{:S(2)}, u32[]{:S(2)}) collective-permute-start(bf16[64,768]{1,0:T(8,128)(2,1)S(1)} %collective-permute-done.19), channel_id=1, source_target_pairs={{0,4},{4,0},{8,12},{12,8},{16,20},{20,16},{24,28},{28,24},{1,5},{5... | collective-permute-start | bytes 294920 | tf_op jit(solution)/shard_map/ppermute | solution.py:16
  15.1 3.3 %collective-permute-start.24 = (bf16[64,768]{1,0:T(8,128)(2,1)S(1)}, bf16[64,768]{1,0:T(8,128)(2,1)S(1)}, u32[]{:S(2)}, u32[]{:S(2)}) collective-permute-start(bf16[64,768]{1,0:T(8,128)(2,1)S(1)} %collective-permute-done.20), channel_id=1, source_target_pairs={{0,4},{4,0},{8,12},{12,8},{16,20},{20,16},{24,28},{28,24},{1,5},{5... | collective-permute-start | bytes 294920 | tf_op jit(solution)/shard_map/ppermute | solution.py:16
  15.7 1.4 %collective-permute-start.21 = (bf16[64,768]{1,0:T(8,128)(2,1)S(1)}, bf16[64,768]{1,0:T(8,128)(2,1)S(1)}, u32[]{:S(2)}, u32[]{:S(2)}) collective-permute-start(bf16[64,768]{1,0:T(8,128)(2,1)S(1)} %copy-done.3), channel_id=1, source_target_pairs={{0,4},{4,0},{8,12},{12,8},{16,20},{20,16},{24,28},{28,24},{1,5},{5... | collective-permute-start | bytes 294920 | tf_op jit(solution)/shard_map/ppermute | solution.py:16
  16.4 0.9 %copy-start.2 = (bf16[128,768]{1,0:T(8,128)(2,1)S(1)}, bf16[128,768]{1,0:T(8,128)(2,1)}, u32[]{:S(2)}) copy-start(bf16[128,768]{1,0:T(8,128)(2,1)} %param.5) | copy-start | bytes 589828
  17.3 2.5 %collective-permute-start.26 = (bf16[128,768]{1,0:T(8,128)(2,1)S(1)}, bf16[128,768]{1,0:T(8,128)(2,1)S(1)}, u32[]{:S(2)}, u32[]{:S(2)}) collective-permute-start(bf16[128,768]{1,0:T(8,128)(2,1)S(1)} %copy-done.2), channel_id=1, source_target_pairs={{0,4},{4,0},{8,12},{12,8},{16,20},{20,16},{24,28},{28,24},{1,5},{5... | collective-permute-start | bytes 589832 | tf_op jit(solution)/shard_map/ppermute | solution.py:16
  17.8 2.0 %collective-permute-start.27 = (bf16[128,768]{1,0:T(8,128)(2,1)S(1)}, bf16[128,768]{1,0:T(8,128)(2,1)S(1)}, u32[]{:S(2)}, u32[]{:S(2)}) collective-permute-start(bf16[128,768]{1,0:T(8,128)(2,1)S(1)} %collective-permute-done.15), channel_id=1, source_target_pairs={{0,4},{4,0},{8,12},{12,8},{16,20},{20,16},{24,28},{28,24},{1,5},{5... | collective-permute-start | bytes 589832 | tf_op jit(solution)/shard_map/ppermute | solution.py:16
  18.0 1.9 %collective-permute-start.28 = (bf16[128,768]{1,0:T(8,128)(2,1)S(1)}, bf16[128,768]{1,0:T(8,128)(2,1)S(1)}, u32[]{:S(2)}, u32[]{:S(2)}) collective-permute-start(bf16[128,768]{1,0:T(8,128)(2,1)S(1)} %collective-permute-done.16), channel_id=1, source_target_pairs={{0,4},{4,0},{8,12},{12,8},{16,20},{20,16},{24,28},{28,24},{1,5},{5... | collective-permute-start | bytes 589832 | tf_op jit(solution)/shard_map/ppermute | solution.py:16
  19.7 1.4 %collective-permute-start.29 = (bf16[128,768]{1,0:T(8,128)(2,1)S(1)}, bf16[128,768]{1,0:T(8,128)(2,1)S(1)}, u32[]{:S(2)}, u32[]{:S(2)}) collective-permute-start(bf16[128,768]{1,0:T(8,128)(2,1)S(1)} %collective-permute-done.17), channel_id=1, source_target_pairs={{0,4},{4,0},{8,12},{12,8},{16,20},{20,16},{24,28},{28,24},{1,5},{5... | collective-permute-start | bytes 589832 | tf_op jit(solution)/shard_map/ppermute | solution.py:16
  21.2 0.9 %copy-start = (bf16[512,768]{1,0:T(8,128)(2,1)}, bf16[512,768]{1,0:T(8,128)(2,1)S(1)}, u32[]{:S(2)}) copy-start(bf16[512,768]{1,0:T(8,128)(2,1)S(1)} %constant_dynamic-update-slice_fusion.52) | copy-start | bytes 2359300
  22.1 30.2 %collective-permute-start.30 = (f32[3,512]{1,0:T(4,128)S(1)}, f32[3,512]{1,0:T(4,128)S(1)}, u32[]{:S(2)}, u32[]{:S(2)}) collective-permute-start(f32[3,512]{1,0:T(4,128)S(1)} %get-tuple-element.102), channel_id=1, source_target_pairs={{0,4},{4,0},{8,12},{12,8},{16,20},{20,16},{24,28},{28,24},{1,5},{5... | collective-permute-start | bytes 18440 | tf_op jit(solution)/shard_map/ppermute | solution.py:16
  52.9 1.1 %copy-start.1 = (bf16[512,768]{1,0:T(8,128)(2,1)S(1)}, bf16[512,768]{1,0:T(8,128)(2,1)}, u32[]{:S(2)}) copy-start(bf16[512,768]{1,0:T(8,128)(2,1)} %copy-done) | copy-start | bytes 2359300
  54.5 5.4 %collective-permute-start.31 = (bf16[72,768]{1,0:T(8,128)(2,1)S(1)}, bf16[72,768]{1,0:T(8,128)(2,1)S(1)}, u32[]{:S(2)}, u32[]{:S(2)}) collective-permute-start(bf16[72,768]{1,0:T(8,128)(2,1)S(1)} %get-tuple-element.88), channel_id=1, source_target_pairs={{0,8},{4,12},{8,0},{12,4},{16,24},{20,28},{24,16},{28,20},{1,9},{5... | collective-permute-start | bytes 331784 | tf_op jit(solution)/shard_map/ppermute | solution.py:16
  56.6 11.3 %collective-permute-start.32 = (bf16[72,768]{1,0:T(8,128)(2,1)S(1)}, bf16[72,768]{1,0:T(8,128)(2,1)S(1)}, u32[]{:S(2)}, u32[]{:S(2)}) collective-permute-start(bf16[72,768]{1,0:T(8,128)(2,1)S(1)} %get-tuple-element.89), channel_id=1, source_target_pairs={{0,16},{4,20},{8,24},{12,28},{16,0},{20,4},{24,8},{28,12},{1,17},{... | collective-permute-start | bytes 331784 | tf_op jit(solution)/shard_map/ppermute | solution.py:16
  57.8 10.1 %collective-permute-start.33 = (bf16[72,768]{1,0:T(8,128)(2,1)S(1)}, bf16[72,768]{1,0:T(8,128)(2,1)S(1)}, u32[]{:S(2)}, u32[]{:S(2)}) collective-permute-start(bf16[72,768]{1,0:T(8,128)(2,1)S(1)} %get-tuple-element.90), channel_id=1, source_target_pairs={{0,24},{4,28},{8,16},{12,20},{16,8},{20,12},{24,0},{28,4},{1,25},{... | collective-permute-start | bytes 331784 | tf_op jit(solution)/shard_map/ppermute | solution.py:16

commit v2 on v1

--- a/solution.py
+++ b/solution.py
@@ -34,13 +34,11 @@
 
 
 def gather_spans(x, core):
-    first = None
     parts = [x]
     ready = x
     for at, size in stages("col"):
         x = jnp.concatenate(parts)
         parts = [x] + [swap(x, "col", d << at) for d in range(1, min(size, 3))]
-        first = parts[1] if first is None else first
         near = parts
         if size == 4:
             passed_on = jnp.where(core == 1, parts[2], parts[1])
@@ -48,7 +46,7 @@
             ready = passed_on
             parts = parts + [swap_by_core(passed_on, "col", (2 << at, 1 << at))]
     mate = [swap(part, "row", 1) for part in near + parts[3:]]
-    return parts, mate, first, ready
+    return parts, mate, ready
 
 
 def after(x, other):
@@ -62,10 +60,11 @@
     return whole.reshape((-1,) + parts[0].shape[1:])
 
 
-def gather_centroids(x, ready):
+def gather_centroids(x, first, ready):
     for at, size in stages("row"):
-        parts = [x] + [after(swap(x, "row", d << at), ready) for d in range(1, size)]
-        mate = [swap(after(part, ready) if part is x else part, "row", 1) for part in parts]
+        sent = after(x, first)
+        parts = [sent] + [after(swap(sent, "row", d << at), ready) for d in range(1, size)]
+        mate = [swap(after(part, ready) if part is sent else part, "row", 1) for part in parts]
         position = digit("row", at, size)
         x = placed(parts, position)
     return jnp.concatenate([x, placed(mate, position)])
@@ -152,9 +151,10 @@
     mass_ratio = group_cols * cols / (row_count * rows)
     target = 1 / mass_ratio
 
-    own_parts, mate_parts, first, ready = gather_spans(spans, core)
-    mate_pattern = swap(after(pattern, first), "row", 1)
-    tile_centroids = gather_centroids(centroids, ready)
+    mate_pattern = swap(pattern, "row", 1)
+    own_parts, mate_parts, ready = gather_spans(spans, core)
+    tile_centroids = gather_centroids(centroids, mate_pattern, ready)
+    own_parts = [after(own_parts[0], mate_pattern)] + own_parts[1:]
     span_halves = [jnp.concatenate(own_parts), jnp.concatenate(mate_parts)]
     at = jnp.arange(group_cols)
     row_of = at % half_cols // per * 2 + (at // half_cols ^ core)

time: 70.4 us -> 71 us (level)
  waiting for transfers between devices: 14.1 us -> 17.6 us
  starting transfers between devices: 45.5 us -> 43.6 us
  local copies, waits for them, and re-layouts: 4.6 us -> 3.08 us
    ppermute x18, waiting for transfers between devices: 12.9 us -> 17.6 us  [swap(): lax.ppermute(x, axis, [(i, i ^ k) for i in range(lax.axis_size(axis))])]
    ppermute x18, starting transfers between devices: 45 us -> 43.1 us  [swap(): lax.ppermute(x, axis, [(i, i ^ k) for i in range(lax.axis_size(axis))])]
    ppermute x1, waiting for transfers between devices: 1.22 us -> 0.01 us  [swap_by_core(): return lax.ppermute(x, ('row', 'col'), pairs)]
    dynamic_update_slice x8, local copies, waits for them, and re-layouts: 1.05 us -> 0.1 us  [placed(): whole = lax.dynamic_update_index_in_dim(whole, part, index ^ d, 0)]
    unnamed x17 -> x15, local copies, waits for them, and re-layouts: 2.28 us -> 1.71 us
  transfers between devices with their start and end apart: 19 -> 19, of which waited for: 8 -> 10; matrix products, arithmetic and copies ran while one was open for 6% -> 4% of each run, Pallas kernels for 0% -> 0%
where the time goes in v2:
time: 71 us; the launch traced here: 70.8 us
  starting transfers between devices  43.6 us (61%)
  waiting for transfers between devices  17.6 us (25%)
  local copies, waits for them, and re-layouts  3.08 us (4%)
  other arithmetic  2.91 us (4%)
  matrix products  2.57 us (4%)
  between operations  1.05 us (1%)
    ppermute x18, starting transfers between devices, swap(): lax.ppermute(x, axis, [(i, i ^ k) for i in range(lax.axis_size(axis))])  43.1 us
    ppermute x18, waiting for transfers between devices, swap(): lax.ppermute(x, axis, [(i, i ^ k) for i in range(lax.axis_size(axis))])  17.6 us
    unnamed x15, local copies, waits for them, and re-layouts  1.71 us
  transfers between devices with their start and end apart: 19, of which 10 were waited for; matrix products, arithmetic and copies ran while one was open for 4% of the time, Pallas kernels for 0%

profile of v2, /device:TPU:0, one launch (start us, length us, event | category | flops | bytes accessed | tf_op | source)
XLA Modules:
  0.0 70.8 jit_solution(13649799161223162703)
XLA Ops:
  0.6 3.0 %collective-permute-start.16 = (bf16[128,768]{1,0:T(8,128)(2,1)}, bf16[128,768]{1,0:T(8,128)(2,1)S(1)}, u32[]{:S(2)}, u32[]{:S(2)}) collective-permute-start(bf16[128,768]{1,0:T(8,128)(2,1)} %param.5), channel_id=1, source_target_pairs={{0,1},{1,0},{2,3},{3,2},{4,5},{5,4},{6,7},{7,6},{8,9},{9,8},{10,11... | collective-permute-start | bytes 589832 | tf_op jit(solution)/shard_map/ppermute | solution.py:16
  3.6 1.5 %collective-permute-start.17 = (bf16[128,768]{1,0:T(8,128)(2,1)}, bf16[128,768]{1,0:T(8,128)(2,1)S(1)}, u32[]{:S(2)}, u32[]{:S(2)}) collective-permute-start(bf16[128,768]{1,0:T(8,128)(2,1)} %param.5), channel_id=1, source_target_pairs={{0,2},{1,3},{2,0},{3,1},{4,6},{5,7},{6,4},{7,5},{8,10},{9,11},{10,... | collective-permute-start | bytes 589832 | tf_op jit(solution)/shard_map/ppermute | solution.py:16
  5.2 1.3 %collective-permute-done.15 = s32[4,4]{1,0:T(4,128)S(1)} collective-permute-done((s32[4,4]{1,0:T(4,128)}, s32[4,4]{1,0:T(4,128)S(1)}, u32[]{:S(2)}, u32[]{:S(2)}) %collective-permute-start.15) | collective-permute-done | bytes 96 | tf_op jit(solution)/shard_map/ppermute | solution.py:16
  6.5 3.6 %collective-permute-start.21 = (bf16[64,768]{1,0:T(8,128)(2,1)}, bf16[64,768]{1,0:T(8,128)(2,1)S(1)}, u32[]{:S(2)}, u32[]{:S(2)}) collective-permute-start(bf16[64,768]{1,0:T(8,128)(2,1)} %param.6), channel_id=1, source_target_pairs={{0,24},{4,28},{8,16},{12,20},{16,8},{20,12},{24,0},{28,4},{1,25},{... | collective-permute-start | bytes 294920 | tf_op jit(solution)/shard_map/ppermute | solution.py:16
  10.1 0.8 %collective-permute-start.19 = (bf16[64,768]{1,0:T(8,128)(2,1)}, bf16[64,768]{1,0:T(8,128)(2,1)S(1)}, u32[]{:S(2)}, u32[]{:S(2)}) collective-permute-start(bf16[64,768]{1,0:T(8,128)(2,1)} %param.6), channel_id=1, source_target_pairs={{0,8},{4,12},{8,0},{12,4},{16,24},{20,28},{24,16},{28,20},{1,9},{5... | collective-permute-start | bytes 294920 | tf_op jit(solution)/shard_map/ppermute | solution.py:16
  10.9 0.8 %compare_reduce_fusion = (pred[4,4]{1,0:T(4,128)(4,1)S(1)}, pred[4,4]{1,0:T(4,128)(4,1)S(1)}) fusion(s32[4,4]{1,0:T(4,128)S(1)} %collective-permute-done.15, s32[4]{0:T(128)S(1)} %iota_add_fusion, s32[4,4]{1,0:T(4,128)} %param.7), kind=kLoop, calls=%fused_computation.140 | loop fusion | flops 224 | bytes 176 | tf_op jit(solution)/shard_map/reduce_or | solution.py:165
  12.4 0.6 copy-done.2
  13.2 0.6 collective-permute-start.18
  13.8 0.5 collective-permute-done.21
  14.3 4.7 %collective-permute-done.20 = bf16[64,768]{1,0:T(8,128)(2,1)S(1)} collective-permute-done((bf16[64,768]{1,0:T(8,128)(2,1)}, bf16[64,768]{1,0:T(8,128)(2,1)S(1)}, u32[]{:S(2)}, u32[]{:S(2)}) %collective-permute-start.20) | collective-permute-done | bytes 98336 | tf_op jit(solution)/shard_map/ppermute | solution.py:16
  18.9 0.5 collective-permute-start.24
  19.5 0.5 collective-permute-start.22
  20.0 0.9 %collective-permute-done.22 = bf16[64,768]{1,0:T(8,128)(2,1)S(1)} collective-permute-done((bf16[64,768]{1,0:T(8,128)(2,1)S(1)}, bf16[64,768]{1,0:T(8,128)(2,1)S(1)}, u32[]{:S(2)}, u32[]{:S(2)}) %collective-permute-start.22) | collective-permute-done | bytes 98336 | tf_op jit(solution)/shard_map/ppermute | solution.py:16
  20.9 0.4 collective-permute-start.26
  21.6 0.4 collective-permute-start.28
  22.4 0.5 collective-permute-done.27
  23.1 0.6 fusion.10
  23.8 0.6 fusion.11
  24.7 27.5 %collective-permute-start.30 = (f32[3,512]{1,0:T(4,128)S(1)}, f32[3,512]{1,0:T(4,128)S(1)}, u32[]{:S(2)}, u32[]{:S(2)}) collective-permute-start(f32[3,512]{1,0:T(4,128)S(1)} %get-tuple-element.104), channel_id=1, source_target_pairs={{0,4},{4,0},{8,12},{12,8},{16,20},{20,16},{24,28},{28,24},{1,5},{5... | collective-permute-start | bytes 18440 | tf_op jit(solution)/shard_map/ppermute | solution.py:16
  52.2 0.8 %collective-permute-done.30 = f32[3,512]{1,0:T(4,128)S(1)} collective-permute-done((f32[3,512]{1,0:T(4,128)S(1)}, f32[3,512]{1,0:T(4,128)S(1)}, u32[]{:S(2)}, u32[]{:S(2)}) %collective-permute-start.30) | collective-permute-done | bytes 6176 | tf_op jit(solution)/shard_map/ppermute | solution.py:16
  53.1 0.4 exponential_reduce_fusion.10
  53.6 0.4 fusion.16
  54.0 0.7 %copy-done.1 = bf16[512,768]{1,0:T(8,128)(2,1)S(1)} copy-done((bf16[512,768]{1,0:T(8,128)(2,1)S(1)}, bf16[512,768]{1,0:T(8,128)(2,1)}, u32[]{:S(2)}) %copy-start.1) | copy-done | bytes 786456
  54.7 0.4 convolution_add_fusion
  55.2 1.8 %collective-permute-start.31 = (bf16[72,768]{1,0:T(8,128)(2,1)S(1)}, bf16[72,768]{1,0:T(8,128)(2,1)S(1)}, u32[]{:S(2)}, u32[]{:S(2)}) collective-permute-start(bf16[72,768]{1,0:T(8,128)(2,1)S(1)} %get-tuple-element.90), channel_id=1, source_target_pairs={{0,8},{4,12},{8,0},{12,4},{16,24},{20,28},{24,16},{28,20},{1,9},{5... | collective-permute-start | bytes 331784 | tf_op jit(solution)/shard_map/ppermute | solution.py:16
  57.3 1.2 %collective-permute-start.32 = (bf16[72,768]{1,0:T(8,128)(2,1)S(1)}, bf16[72,768]{1,0:T(8,128)(2,1)S(1)}, u32[]{:S(2)}, u32[]{:S(2)}) collective-permute-start(bf16[72,768]{1,0:T(8,128)(2,1)S(1)} %get-tuple-element.91), channel_id=1, source_target_pairs={{0,16},{4,20},{8,24},{12,28},{16,0},{20,4},{24,8},{28,12},{1,17},{... | collective-permute-start | bytes 331784 | tf_op jit(solution)/shard_map/ppermute | solution.py:16
  58.5 1.5 %collective-permute-start.33 = (bf16[72,768]{1,0:T(8,128)(2,1)S(1)}, bf16[72,768]{1,0:T(8,128)(2,1)S(1)}, u32[]{:S(2)}, u32[]{:S(2)}) collective-permute-start(bf16[72,768]{1,0:T(8,128)(2,1)S(1)} %get-tuple-element.92), channel_id=1, source_target_pairs={{0,24},{4,28},{8,16},{12,20},{16,8},{20,12},{24,0},{28,4},{1,25},{... | collective-permute-start | bytes 331784 | tf_op jit(solution)/shard_map/ppermute | solution.py:16
  59.9 0.7 collective-permute-done.31
  60.6 7.9 %collective-permute-done.32 = bf16[72,768]{1,0:T(8,128)(2,1)S(1)} collective-permute-done((bf16[72,768]{1,0:T(8,128)(2,1)S(1)}, bf16[72,768]{1,0:T(8,128)(2,1)S(1)}, u32[]{:S(2)}, u32[]{:S(2)}) %collective-permute-start.32) | collective-permute-done | bytes 110624 | tf_op jit(solution)/shard_map/ppermute | solution.py:16
  68.8 0.7 reshape.496
  69.5 0.6 pad_maximum_fusion.9
  70.1 0.7 %fusion.24 = bf16[64,768]{1,0:T(8,128)(2,1)} fusion(f32[1,4,64,768]{3,2,1,0:T(8,128)S(1)} %bitcast.67, s32[]{:T(128)S(6)} %select_n.199, bf16[72,768]{1,0:T(8,128)(2,1)S(1)} %collective-permute-done.33, bf16[72,768]{1,0:T(8,128)(2,1)S(1)} %collective-permute-done.32, bf16[72,768]{1,0:T(8,128)(2,1)S(1)} %collective-permute-done.31, f32[64]{0:T(128)S(1)} %fusion.58), kind=kLoop, calls=%fused_computation.115 | loop fusion | flops 393216 | bytes 590084 | tf_op jit(solution)/shard_map/convert_element_type | solution.py:239
  (84 shorter events, 2.8 us)
Async XLA Ops:
  0.6 12.5 %collective-permute-start.16 = (bf16[128,768]{1,0:T(8,128)(2,1)}, bf16[128,768]{1,0:T(8,128)(2,1)S(1)}, u32[]{:S(2)}, u32[]{:S(2)}) collective-permute-start(bf16[128,768]{1,0:T(8,128)(2,1)} %param.5), channel_id=1, source_target_pairs={{0,1},{1,0},{2,3},{3,2},{4,5},{5,4},{6,7},{7,6},{8,9},{9,8},{10,11... | collective-permute-start | bytes 589832 | tf_op jit(solution)/shard_map/ppermute | solution.py:16
  3.6 9.5 %collective-permute-start.17 = (bf16[128,768]{1,0:T(8,128)(2,1)}, bf16[128,768]{1,0:T(8,128)(2,1)S(1)}, u32[]{:S(2)}, u32[]{:S(2)}) collective-permute-start(bf16[128,768]{1,0:T(8,128)(2,1)} %param.5), channel_id=1, source_target_pairs={{0,2},{1,3},{2,0},{3,1},{4,6},{5,7},{6,4},{7,5},{8,10},{9,11},{10,... | collective-permute-start | bytes 589832 | tf_op jit(solution)/shard_map/ppermute | solution.py:16
  5.2 1.4 %collective-permute-start.15 = (s32[4,4]{1,0:T(4,128)}, s32[4,4]{1,0:T(4,128)S(1)}, u32[]{:S(2)}, u32[]{:S(2)}) collective-permute-start(s32[4,4]{1,0:T(4,128)} %param.7), channel_id=1, source_target_pairs={{0,4},{4,0},{8,12},{12,8},{16,20},{20,16},{24,28},{28,24},{1,5},{5... | collective-permute-start | bytes 200 | tf_op jit(solution)/shard_map/ppermute | solution.py:16
  6.5 7.7 %collective-permute-start.21 = (bf16[64,768]{1,0:T(8,128)(2,1)}, bf16[64,768]{1,0:T(8,128)(2,1)S(1)}, u32[]{:S(2)}, u32[]{:S(2)}) collective-permute-start(bf16[64,768]{1,0:T(8,128)(2,1)} %param.6), channel_id=1, source_target_pairs={{0,24},{4,28},{8,16},{12,20},{16,8},{20,12},{24,0},{28,4},{1,25},{... | collective-permute-start | bytes 294920 | tf_op jit(solution)/shard_map/ppermute | solution.py:16
  10.1 8.8 %collective-permute-start.20 = (bf16[64,768]{1,0:T(8,128)(2,1)}, bf16[64,768]{1,0:T(8,128)(2,1)S(1)}, u32[]{:S(2)}, u32[]{:S(2)}) collective-permute-start(bf16[64,768]{1,0:T(8,128)(2,1)} %param.6), channel_id=1, source_target_pairs={{0,16},{4,20},{8,24},{12,28},{16,0},{20,4},{24,8},{28,12},{1,17},{... | collective-permute-start | bytes 294920 | tf_op jit(solution)/shard_map/ppermute | solution.py:16
  10.1 8.8 %collective-permute-start.19 = (bf16[64,768]{1,0:T(8,128)(2,1)}, bf16[64,768]{1,0:T(8,128)(2,1)S(1)}, u32[]{:S(2)}, u32[]{:S(2)}) collective-permute-start(bf16[64,768]{1,0:T(8,128)(2,1)} %param.6), channel_id=1, source_target_pairs={{0,8},{4,12},{8,0},{12,4},{16,24},{20,28},{24,16},{28,20},{1,9},{5... | collective-permute-start | bytes 294920 | tf_op jit(solution)/shard_map/ppermute | solution.py:16
  12.1 0.9 %copy-start.2 = (bf16[128,768]{1,0:T(8,128)(2,1)S(1)}, bf16[128,768]{1,0:T(8,128)(2,1)}, u32[]{:S(2)}) copy-start(bf16[128,768]{1,0:T(8,128)(2,1)} %param.5) | copy-start | bytes 589828
  12.1 1.0 %copy-start.3 = (bf16[64,768]{1,0:T(8,128)(2,1)S(1)}, bf16[64,768]{1,0:T(8,128)(2,1)}, u32[]{:S(2)}) copy-start(bf16[64,768]{1,0:T(8,128)(2,1)} %param.6) | copy-start | bytes 294916
  13.2 8.8 %collective-permute-start.18 = (bf16[128,768]{1,0:T(8,128)(2,1)S(1)}, bf16[128,768]{1,0:T(8,128)(2,1)S(1)}, u32[]{:S(2)}, u32[]{:S(2)}) collective-permute-start(bf16[128,768]{1,0:T(8,128)(2,1)S(1)} %get-tuple-element.81), channel_id=1, source_target_pairs={{0,2},{1,3},{2,0},{3,1},{4,5},{5,4},{6,7},{7,6},{8,10},{9,11},{10,... | collective-permute-start | bytes 589832 | tf_op jit(solution)/shard_map/ppermute | solution.py:23
  18.9 2.4 %collective-permute-start.23 = (bf16[64,768]{1,0:T(8,128)(2,1)S(1)}, bf16[64,768]{1,0:T(8,128)(2,1)S(1)}, u32[]{:S(2)}, u32[]{:S(2)}) collective-permute-start(bf16[64,768]{1,0:T(8,128)(2,1)S(1)} %collective-permute-done.19), channel_id=1, source_target_pairs={{0,4},{4,0},{8,12},{12,8},{16,20},{20,16},{24,28},{28,24},{1,5},{5... | collective-permute-start | bytes 294920 | tf_op jit(solution)/shard_map/ppermute | solution.py:16
  18.9 2.6 %collective-permute-start.24 = (bf16[64,768]{1,0:T(8,128)(2,1)S(1)}, bf16[64,768]{1,0:T(8,128)(2,1)S(1)}, u32[]{:S(2)}, u32[]{:S(2)}) collective-permute-start(bf16[64,768]{1,0:T(8,128)(2,1)S(1)} %collective-permute-done.20), channel_id=1, source_target_pairs={{0,4},{4,0},{8,12},{12,8},{16,20},{20,16},{24,28},{28,24},{1,5},{5... | collective-permute-start | bytes 294920 | tf_op jit(solution)/shard_map/ppermute | solution.py:16
  19.5 2.6 %collective-permute-start.25 = (bf16[64,768]{1,0:T(8,128)(2,1)S(1)}, bf16[64,768]{1,0:T(8,128)(2,1)S(1)}, u32[]{:S(2)}, u32[]{:S(2)}) collective-permute-start(bf16[64,768]{1,0:T(8,128)(2,1)S(1)} %collective-permute-done.21), channel_id=1, source_target_pairs={{0,4},{4,0},{8,12},{12,8},{16,20},{20,16},{24,28},{28,24},{1,5},{5... | collective-permute-start | bytes 294920 | tf_op jit(solution)/shard_map/ppermute | solution.py:16
  19.5 1.5 %collective-permute-start.22 = (bf16[64,768]{1,0:T(8,128)(2,1)S(1)}, bf16[64,768]{1,0:T(8,128)(2,1)S(1)}, u32[]{:S(2)}, u32[]{:S(2)}) collective-permute-start(bf16[64,768]{1,0:T(8,128)(2,1)S(1)} %copy-done.3), channel_id=1, source_target_pairs={{0,4},{4,0},{8,12},{12,8},{16,20},{20,16},{24,28},{28,24},{1,5},{5... | collective-permute-start | bytes 294920 | tf_op jit(solution)/shard_map/ppermute | solution.py:16
  20.9 1.4 %collective-permute-start.26 = (bf16[128,768]{1,0:T(8,128)(2,1)S(1)}, bf16[128,768]{1,0:T(8,128)(2,1)S(1)}, u32[]{:S(2)}, u32[]{:S(2)}) collective-permute-start(bf16[128,768]{1,0:T(8,128)(2,1)S(1)} %copy-done.2), channel_id=1, source_target_pairs={{0,4},{4,0},{8,12},{12,8},{16,20},{20,16},{24,28},{28,24},{1,5},{5... | collective-permute-start | bytes 589832 | tf_op jit(solution)/shard_map/ppermute | solution.py:16
  21.3 1.5 %collective-permute-start.27 = (bf16[128,768]{1,0:T(8,128)(2,1)S(1)}, bf16[128,768]{1,0:T(8,128)(2,1)S(1)}, u32[]{:S(2)}, u32[]{:S(2)}) collective-permute-start(bf16[128,768]{1,0:T(8,128)(2,1)S(1)} %collective-permute-done.16), channel_id=1, source_target_pairs={{0,4},{4,0},{8,12},{12,8},{16,20},{20,16},{24,28},{28,24},{1,5},{5... | collective-permute-start | bytes 589832 | tf_op jit(solution)/shard_map/ppermute | solution.py:16
  21.6 1.5 %collective-permute-start.28 = (bf16[128,768]{1,0:T(8,128)(2,1)S(1)}, bf16[128,768]{1,0:T(8,128)(2,1)S(1)}, u32[]{:S(2)}, u32[]{:S(2)}) collective-permute-start(bf16[128,768]{1,0:T(8,128)(2,1)S(1)} %collective-permute-done.17), channel_id=1, source_target_pairs={{0,4},{4,0},{8,12},{12,8},{16,20},{20,16},{24,28},{28,24},{1,5},{5... | collective-permute-start | bytes 589832 | tf_op jit(solution)/shard_map/ppermute | solution.py:16
  22.1 1.7 %collective-permute-start.29 = (bf16[128,768]{1,0:T(8,128)(2,1)S(1)}, bf16[128,768]{1,0:T(8,128)(2,1)S(1)}, u32[]{:S(2)}, u32[]{:S(2)}) collective-permute-start(bf16[128,768]{1,0:T(8,128)(2,1)S(1)} %collective-permute-done.18), channel_id=1, source_target_pairs={{0,4},{4,0},{8,12},{12,8},{16,20},{20,16},{24,28},{28,24},{1,5},{5... | collective-permute-start | bytes 589832 | tf_op jit(solution)/shard_map/ppermute | solution.py:16
  23.8 0.9 %copy-start = (bf16[512,768]{1,0:T(8,128)(2,1)}, bf16[512,768]{1,0:T(8,128)(2,1)S(1)}, u32[]{:S(2)}) copy-start(bf16[512,768]{1,0:T(8,128)(2,1)S(1)} %constant_dynamic-update-slice_fusion.52) | copy-start | bytes 2359300
  24.7 28.3 %collective-permute-start.30 = (f32[3,512]{1,0:T(4,128)S(1)}, f32[3,512]{1,0:T(4,128)S(1)}, u32[]{:S(2)}, u32[]{:S(2)}) collective-permute-start(f32[3,512]{1,0:T(4,128)S(1)} %get-tuple-element.104), channel_id=1, source_target_pairs={{0,4},{4,0},{8,12},{12,8},{16,20},{20,16},{24,28},{28,24},{1,5},{5... | collective-permute-start | bytes 18440 | tf_op jit(solution)/shard_map/ppermute | solution.py:16
  53.6 1.1 %copy-start.1 = (bf16[512,768]{1,0:T(8,128)(2,1)S(1)}, bf16[512,768]{1,0:T(8,128)(2,1)}, u32[]{:S(2)}) copy-start(bf16[512,768]{1,0:T(8,128)(2,1)} %copy-done) | copy-start | bytes 2359300
  55.2 5.4 %collective-permute-start.31 = (bf16[72,768]{1,0:T(8,128)(2,1)S(1)}, bf16[72,768]{1,0:T(8,128)(2,1)S(1)}, u32[]{:S(2)}, u32[]{:S(2)}) collective-permute-start(bf16[72,768]{1,0:T(8,128)(2,1)S(1)} %get-tuple-element.90), channel_id=1, source_target_pairs={{0,8},{4,12},{8,0},{12,4},{16,24},{20,28},{24,16},{28,20},{1,9},{5... | collective-permute-start | bytes 331784 | tf_op jit(solution)/shard_map/ppermute | solution.py:16
  57.3 11.3 %collective-permute-start.32 = (bf16[72,768]{1,0:T(8,128)(2,1)S(1)}, bf16[72,768]{1,0:T(8,128)(2,1)S(1)}, u32[]{:S(2)}, u32[]{:S(2)}) collective-permute-start(bf16[72,768]{1,0:T(8,128)(2,1)S(1)} %get-tuple-element.91), channel_id=1, source_target_pairs={{0,16},{4,20},{8,24},{12,28},{16,0},{20,4},{24,8},{28,12},{1,17},{... | collective-permute-start | bytes 331784 | tf_op jit(solution)/shard_map/ppermute | solution.py:16
  58.5 10.1 %collective-permute-start.33 = (bf16[72,768]{1,0:T(8,128)(2,1)S(1)}, bf16[72,768]{1,0:T(8,128)(2,1)S(1)}, u32[]{:S(2)}, u32[]{:S(2)}) collective-permute-start(bf16[72,768]{1,0:T(8,128)(2,1)S(1)} %get-tuple-element.92), channel_id=1, source_target_pairs={{0,24},{4,28},{8,16},{12,20},{16,8},{20,12},{24,0},{28,4},{1,25},{... | collective-permute-start | bytes 331784 | tf_op jit(solution)/shard_map/ppermute | solution.py:16

commit v3 on v1

--- a/solution.py
+++ b/solution.py
@@ -48,7 +48,7 @@
             ready = passed_on
             parts = parts + [swap_by_core(passed_on, "col", (2 << at, 1 << at))]
     mate = [swap(part, "row", 1) for part in near + parts[3:]]
-    return parts, mate, first, ready
+    return near[:1] + parts[1:], mate, first, ready
 
 
 def after(x, other):
@@ -64,8 +64,9 @@
 
 def gather_centroids(x, ready):
     for at, size in stages("row"):
-        parts = [x] + [after(swap(x, "row", d << at), ready) for d in range(1, size)]
-        mate = [swap(after(part, ready) if part is x else part, "row", 1) for part in parts]
+        sent = after(x, ready)
+        parts = [sent] + [after(swap(x, "row", d << at), ready) for d in range(1, size)]
+        mate = [swap(part, "row", 1) for part in parts]
         position = digit("row", at, size)
         x = placed(parts, position)
     return jnp.concatenate([x, placed(mate, position)])
@@ -205,18 +206,17 @@
     row_pot = jnp.where(core == 1, known[:-1].reshape(-1), reorder(got[:-1].reshape(-1), 2, 1))
     col_pot = jnp.where(core == 1, known[-1], reorder(got[-1], 2, 1))
 
-    mass = col_sums(row_pot, col_pot)
-    held = add(
-        [
-            lax.dot_general(
-                jnp.exp(x[:, :half_cols] + col_pot[None, :half_cols]).astype(jnp.bfloat16),
-                span_half,
-                (((0,), (0,)), ((), ())),
-                preferred_element_type=jnp.float32,
-            )
-            for x, span_half in zip(with_rows(row_pot), span_halves)
-        ]
-    ).reshape(chips, per, width)
+    halves = [
+        lax.dot_general(
+            jnp.exp(x[:, :half_cols] + col_pot[None, :half_cols]).astype(jnp.bfloat16),
+            span_half,
+            (((0,), (0,)), ((), ())),
+            preferred_element_type=jnp.float32,
+        )
+        for x, span_half in zip(with_rows(row_pot), span_halves)
+    ]
+    mass = col_sums(after(row_pot, halves[1]), col_pot)
+    held = add(halves).reshape(chips, per, width)
     for at, size in stages("row"):
         me = digit("row", at, size)
         held = held.reshape((-1, size) + held.shape[1:])

time: 70.4 us -> 73.8 us (1.048)
  waiting for transfers between devices: 14.1 us -> 20.6 us
  starting transfers between devices: 45.5 us -> 43.1 us
  local copies, waits for them, and re-layouts: 4.6 us -> 3.83 us
    ppermute x18, waiting for transfers between devices: 12.9 us -> 17.7 us  [swap(): lax.ppermute(x, axis, [(i, i ^ k) for i in range(lax.axis_size(axis))])]
    ppermute x18, starting transfers between devices: 45 us -> 42.6 us  [swap(): lax.ppermute(x, axis, [(i, i ^ k) for i in range(lax.axis_size(axis))])]
    ppermute x1, waiting for transfers between devices: 1.22 us -> 2.89 us  [swap_by_core(): return lax.ppermute(x, ('row', 'col'), pairs)]
    dynamic_update_slice x8, local copies, waits for them, and re-layouts: 1.05 us -> 0.11 us  [placed(): whole = lax.dynamic_update_index_in_dim(whole, part, index ^ d, 0)]
    unnamed x17 -> x18, local copies, waits for them, and re-layouts: 2.28 us -> 2.45 us
  transfers between devices with their start and end apart: 19 -> 19, of which waited for: 8 -> 9; matrix products, arithmetic and copies ran while one was open for 6% -> 4% of each run, Pallas kernels for 0% -> 0%
where the time goes in v3:
time: 73.8 us; the launch traced here: 73.6 us
  starting transfers between devices  43.1 us (58%)
  waiting for transfers between devices  20.6 us (28%)
  local copies, waits for them, and re-layouts  3.83 us (5%)
  matrix products  2.77 us (4%)
  other arithmetic  2.2 us (3%)
  between operations  1.08 us (1%)
    ppermute x18, starting transfers between devices, swap(): lax.ppermute(x, axis, [(i, i ^ k) for i in range(lax.axis_size(axis))])  42.6 us
    ppermute x18, waiting for transfers between devices, swap(): lax.ppermute(x, axis, [(i, i ^ k) for i in range(lax.axis_size(axis))])  17.7 us
    ppermute x1, waiting for transfers between devices, swap_by_core(): return lax.ppermute(x, ('row', 'col'), pairs)  2.89 us
    unnamed x18, local copies, waits for them, and re-layouts  2.45 us
  transfers between devices with their start and end apart: 19, of which 9 were waited for; matrix products, arithmetic and copies ran while one was open for 4% of the time, Pallas kernels for 0%

profile of v3, /device:TPU:0, one launch (start us, length us, event | category | flops | bytes accessed | tf_op | source)
XLA Modules:
  0.0 73.6 jit_solution(6300364848505257509)
XLA Ops:
  0.7 3.0 %collective-permute-start.15 = (bf16[128,768]{1,0:T(8,128)(2,1)}, bf16[128,768]{1,0:T(8,128)(2,1)S(1)}, u32[]{:S(2)}, u32[]{:S(2)}) collective-permute-start(bf16[128,768]{1,0:T(8,128)(2,1)} %param.5), channel_id=1, source_target_pairs={{0,1},{1,0},{2,3},{3,2},{4,5},{5,4},{6,7},{7,6},{8,9},{9,8},{10,11... | collective-permute-start | bytes 589832 | tf_op jit(solution)/shard_map/ppermute | solution.py:16
  3.7 1.5 %collective-permute-start.16 = (bf16[128,768]{1,0:T(8,128)(2,1)}, bf16[128,768]{1,0:T(8,128)(2,1)S(1)}, u32[]{:S(2)}, u32[]{:S(2)}) collective-permute-start(bf16[128,768]{1,0:T(8,128)(2,1)} %param.5), channel_id=1, source_target_pairs={{0,2},{1,3},{2,0},{3,1},{4,6},{5,7},{6,4},{7,5},{8,10},{9,11},{10,... | collective-permute-start | bytes 589832 | tf_op jit(solution)/shard_map/ppermute | solution.py:16
  5.2 1.6 %collective-permute-start.18 = (bf16[64,768]{1,0:T(8,128)(2,1)}, bf16[64,768]{1,0:T(8,128)(2,1)S(1)}, u32[]{:S(2)}, u32[]{:S(2)}) collective-permute-start(bf16[64,768]{1,0:T(8,128)(2,1)} %param.6), channel_id=1, source_target_pairs={{0,8},{4,12},{8,0},{12,4},{16,24},{20,28},{24,16},{28,20},{1,9},{5... | collective-permute-start | bytes 294920 | tf_op jit(solution)/shard_map/ppermute | solution.py:16
  6.8 2.6 %collective-permute-start.19 = (bf16[64,768]{1,0:T(8,128)(2,1)}, bf16[64,768]{1,0:T(8,128)(2,1)S(1)}, u32[]{:S(2)}, u32[]{:S(2)}) collective-permute-start(bf16[64,768]{1,0:T(8,128)(2,1)} %param.6), channel_id=1, source_target_pairs={{0,16},{4,20},{8,24},{12,28},{16,0},{20,4},{24,8},{28,12},{1,17},{... | collective-permute-start | bytes 294920 | tf_op jit(solution)/shard_map/ppermute | solution.py:16
  9.6 0.6 collective-permute-done.16
  10.3 0.6 collective-permute-done.18
  11.0 5.9 %collective-permute-done.19 = bf16[64,768]{1,0:T(8,128)(2,1)S(1)} collective-permute-done((bf16[64,768]{1,0:T(8,128)(2,1)}, bf16[64,768]{1,0:T(8,128)(2,1)S(1)}, u32[]{:S(2)}, u32[]{:S(2)}) %collective-permute-start.19) | collective-permute-done | bytes 98336 | tf_op jit(solution)/shard_map/ppermute | solution.py:16
  16.8 0.5 collective-permute-start.24
  17.4 0.9 %constant_dynamic-update-slice_fusion.51 = bf16[512,768]{1,0:T(8,128)(2,1)S(1)} fusion(bf16[128,768]{1,0:T(8,128)(2,1)} %param.5), kind=kLoop, calls=%fused_computation.136 | loop fusion | bytes 393216
  18.6 1.0 %collective-permute-done.25 = s32[4,4]{1,0:T(4,128)S(1)} collective-permute-done((s32[4,4]{1,0:T(4,128)S(1)}, s32[4,4]{1,0:T(4,128)S(1)}, u32[]{:S(2)}, u32[]{:S(2)}) %collective-permute-start.25) | collective-permute-done | bytes 96 | tf_op jit(solution)/shard_map/ppermute | solution.py:16
  19.5 0.5 collective-permute-start.17
  20.3 0.3 convolution_compare_fusion.1
  20.9 0.6 copy-done.2
  21.6 0.6 collective-permute-start.27
  22.3 2.9 %collective-permute-done.17 = bf16[128,768]{1,0:T(8,128)(2,1)S(1)} collective-permute-done((bf16[128,768]{1,0:T(8,128)(2,1)S(1)}, bf16[128,768]{1,0:T(8,128)(2,1)S(1)}, u32[]{:S(2)}, u32[]{:S(2)}) %collective-permute-start.17) | collective-permute-done | bytes 196640 | tf_op jit(solution)/shard_map/ppermute | solution.py:23
  25.3 0.6 fusion.10
  26.1 0.5 collective-permute-done.29
  26.7 0.6 fusion.11
  27.3 27.9 %collective-permute-start.30 = (f32[3,512]{1,0:T(4,128)S(1)}, f32[3,512]{1,0:T(4,128)S(1)}, u32[]{:S(2)}, u32[]{:S(2)}) collective-permute-start(f32[3,512]{1,0:T(4,128)S(1)} %get-tuple-element.102), channel_id=1, source_target_pairs={{0,4},{4,0},{8,12},{12,8},{16,20},{20,16},{24,28},{28,24},{1,5},{5... | collective-permute-start | bytes 18440 | tf_op jit(solution)/shard_map/ppermute | solution.py:16
  55.2 0.8 %collective-permute-done.30 = f32[3,512]{1,0:T(4,128)S(1)} collective-permute-done((f32[3,512]{1,0:T(4,128)S(1)}, f32[3,512]{1,0:T(4,128)S(1)}, u32[]{:S(2)}, u32[]{:S(2)}) %collective-permute-start.30) | collective-permute-done | bytes 6176 | tf_op jit(solution)/shard_map/ppermute | solution.py:16
  56.2 0.5 fusion.19
  56.7 0.6 copy-done.1
  57.3 0.5 convolution_add_fusion
  57.9 0.4 exponential_reduce_fusion.10
  58.4 1.8 %collective-permute-start.33 = (bf16[72,768]{1,0:T(8,128)(2,1)S(1)}, bf16[72,768]{1,0:T(8,128)(2,1)S(1)}, u32[]{:S(2)}, u32[]{:S(2)}) collective-permute-start(bf16[72,768]{1,0:T(8,128)(2,1)S(1)} %get-tuple-element.88), channel_id=1, source_target_pairs={{0,24},{4,28},{8,16},{12,20},{16,8},{20,12},{24,0},{28,4},{1,25},{... | collective-permute-start | bytes 331784 | tf_op jit(solution)/shard_map/ppermute | solution.py:16
  60.2 0.8 %collective-permute-start.32 = (bf16[72,768]{1,0:T(8,128)(2,1)S(1)}, bf16[72,768]{1,0:T(8,128)(2,1)S(1)}, u32[]{:S(2)}, u32[]{:S(2)}) collective-permute-start(bf16[72,768]{1,0:T(8,128)(2,1)S(1)} %get-tuple-element.87), channel_id=1, source_target_pairs={{0,16},{4,20},{8,24},{12,28},{16,0},{20,4},{24,8},{28,12},{1,17},{... | collective-permute-start | bytes 331784 | tf_op jit(solution)/shard_map/ppermute | solution.py:16
  61.0 1.9 %collective-permute-start.31 = (bf16[72,768]{1,0:T(8,128)(2,1)S(1)}, bf16[72,768]{1,0:T(8,128)(2,1)S(1)}, u32[]{:S(2)}, u32[]{:S(2)}) collective-permute-start(bf16[72,768]{1,0:T(8,128)(2,1)S(1)} %get-tuple-element.86), channel_id=1, source_target_pairs={{0,8},{4,12},{8,0},{12,4},{16,24},{20,28},{24,16},{28,20},{1,9},{5... | collective-permute-start | bytes 331784 | tf_op jit(solution)/shard_map/ppermute | solution.py:16
  63.1 3.2 %collective-permute-done.33 = bf16[72,768]{1,0:T(8,128)(2,1)S(1)} collective-permute-done((bf16[72,768]{1,0:T(8,128)(2,1)S(1)}, bf16[72,768]{1,0:T(8,128)(2,1)S(1)}, u32[]{:S(2)}, u32[]{:S(2)}) %collective-permute-start.33) | collective-permute-done | bytes 110624 | tf_op jit(solution)/shard_map/ppermute | solution.py:16
  66.3 5.1 %collective-permute-done.32 = bf16[72,768]{1,0:T(8,128)(2,1)S(1)} collective-permute-done((bf16[72,768]{1,0:T(8,128)(2,1)S(1)}, bf16[72,768]{1,0:T(8,128)(2,1)S(1)}, u32[]{:S(2)}, u32[]{:S(2)}) %collective-permute-start.32) | collective-permute-done | bytes 110624 | tf_op jit(solution)/shard_map/ppermute | solution.py:16
  71.6 0.7 reshape.498
  72.3 0.6 pad_maximum_fusion.9
  72.9 0.7 fusion.28
  (88 shorter events, 2.2 us)
Async XLA Ops:
  0.6 17.8 %copy-start.3 = (bf16[64,768]{1,0:T(8,128)(2,1)S(1)}, bf16[64,768]{1,0:T(8,128)(2,1)}, u32[]{:S(2)}) copy-start(bf16[64,768]{1,0:T(8,128)(2,1)} %param.6) | copy-start | bytes 294916
  0.6 17.7 %copy-start.4 = (s32[4,4]{1,0:T(4,128)S(1)}, s32[4,4]{1,0:T(4,128)}, u32[]{:S(2)}) copy-start(s32[4,4]{1,0:T(4,128)} %param.7) | copy-start | bytes 196
  0.7 8.9 %collective-permute-start.15 = (bf16[128,768]{1,0:T(8,128)(2,1)}, bf16[128,768]{1,0:T(8,128)(2,1)S(1)}, u32[]{:S(2)}, u32[]{:S(2)}) collective-permute-start(bf16[128,768]{1,0:T(8,128)(2,1)} %param.5), channel_id=1, source_target_pairs={{0,1},{1,0},{2,3},{3,2},{4,5},{5,4},{6,7},{7,6},{8,9},{9,8},{10,11... | collective-permute-start | bytes 589832 | tf_op jit(solution)/shard_map/ppermute | solution.py:16
  3.7 6.6 %collective-permute-start.16 = (bf16[128,768]{1,0:T(8,128)(2,1)}, bf16[128,768]{1,0:T(8,128)(2,1)S(1)}, u32[]{:S(2)}, u32[]{:S(2)}) collective-permute-start(bf16[128,768]{1,0:T(8,128)(2,1)} %param.5), channel_id=1, source_target_pairs={{0,2},{1,3},{2,0},{3,1},{4,6},{5,7},{6,4},{7,5},{8,10},{9,11},{10,... | collective-permute-start | bytes 589832 | tf_op jit(solution)/shard_map/ppermute | solution.py:16
  5.2 5.8 %collective-permute-start.18 = (bf16[64,768]{1,0:T(8,128)(2,1)}, bf16[64,768]{1,0:T(8,128)(2,1)S(1)}, u32[]{:S(2)}, u32[]{:S(2)}) collective-permute-start(bf16[64,768]{1,0:T(8,128)(2,1)} %param.6), channel_id=1, source_target_pairs={{0,8},{4,12},{8,0},{12,4},{16,24},{20,28},{24,16},{28,20},{1,9},{5... | collective-permute-start | bytes 294920 | tf_op jit(solution)/shard_map/ppermute | solution.py:16
  6.8 10.1 %collective-permute-start.19 = (bf16[64,768]{1,0:T(8,128)(2,1)}, bf16[64,768]{1,0:T(8,128)(2,1)S(1)}, u32[]{:S(2)}, u32[]{:S(2)}) collective-permute-start(bf16[64,768]{1,0:T(8,128)(2,1)} %param.6), channel_id=1, source_target_pairs={{0,16},{4,20},{8,24},{12,28},{16,0},{20,4},{24,8},{28,12},{1,17},{... | collective-permute-start | bytes 294920 | tf_op jit(solution)/shard_map/ppermute | solution.py:16
  9.3 7.5 %collective-permute-start.20 = (bf16[64,768]{1,0:T(8,128)(2,1)}, bf16[64,768]{1,0:T(8,128)(2,1)S(1)}, u32[]{:S(2)}, u32[]{:S(2)}) collective-permute-start(bf16[64,768]{1,0:T(8,128)(2,1)} %param.6), channel_id=1, source_target_pairs={{0,24},{4,28},{8,16},{12,20},{16,8},{20,12},{24,0},{28,4},{1,25},{... | collective-permute-start | bytes 294920 | tf_op jit(solution)/shard_map/ppermute | solution.py:16
  10.3 10.6 %collective-permute-start.21 = (bf16[64,768]{1,0:T(8,128)(2,1)}, bf16[64,768]{1,0:T(8,128)(2,1)S(1)}, u32[]{:S(2)}, u32[]{:S(2)}) collective-permute-start(bf16[64,768]{1,0:T(8,128)(2,1)} %param.6), channel_id=1, source_target_pairs={{0,4},{4,0},{8,12},{12,8},{16,20},{20,16},{24,28},{28,24},{1,5},{5... | collective-permute-start | bytes 294920 | tf_op jit(solution)/shard_map/ppermute | solution.py:16
  11.0 10.6 %collective-permute-start.22 = (bf16[64,768]{1,0:T(8,128)(2,1)S(1)}, bf16[64,768]{1,0:T(8,128)(2,1)S(1)}, u32[]{:S(2)}, u32[]{:S(2)}) collective-permute-start(bf16[64,768]{1,0:T(8,128)(2,1)S(1)} %collective-permute-done.18), channel_id=1, source_target_pairs={{0,4},{4,0},{8,12},{12,8},{16,20},{20,16},{24,28},{28,24},{1,5},{5... | collective-permute-start | bytes 294920 | tf_op jit(solution)/shard_map/ppermute | solution.py:16
  16.8 5.3 %collective-permute-start.23 = (bf16[64,768]{1,0:T(8,128)(2,1)S(1)}, bf16[64,768]{1,0:T(8,128)(2,1)S(1)}, u32[]{:S(2)}, u32[]{:S(2)}) collective-permute-start(bf16[64,768]{1,0:T(8,128)(2,1)S(1)} %collective-permute-done.19), channel_id=1, source_target_pairs={{0,4},{4,0},{8,12},{12,8},{16,20},{20,16},{24,28},{28,24},{1,5},{5... | collective-permute-start | bytes 294920 | tf_op jit(solution)/shard_map/ppermute | solution.py:16
  16.8 5.4 %collective-permute-start.24 = (bf16[64,768]{1,0:T(8,128)(2,1)S(1)}, bf16[64,768]{1,0:T(8,128)(2,1)S(1)}, u32[]{:S(2)}, u32[]{:S(2)}) collective-permute-start(bf16[64,768]{1,0:T(8,128)(2,1)S(1)} %collective-permute-done.20), channel_id=1, source_target_pairs={{0,4},{4,0},{8,12},{12,8},{16,20},{20,16},{24,28},{28,24},{1,5},{5... | collective-permute-start | bytes 294920 | tf_op jit(solution)/shard_map/ppermute | solution.py:16
  18.3 1.2 %collective-permute-start.25 = (s32[4,4]{1,0:T(4,128)S(1)}, s32[4,4]{1,0:T(4,128)S(1)}, u32[]{:S(2)}, u32[]{:S(2)}) collective-permute-start(s32[4,4]{1,0:T(4,128)S(1)} %copy-done.4), channel_id=1, source_target_pairs={{0,4},{4,0},{8,12},{12,8},{16,20},{20,16},{24,28},{28,24},{1,5},{5... | collective-permute-start | bytes 200 | tf_op jit(solution)/shard_map/ppermute | solution.py:16
  19.5 5.7 %collective-permute-start.17 = (bf16[128,768]{1,0:T(8,128)(2,1)S(1)}, bf16[128,768]{1,0:T(8,128)(2,1)S(1)}, u32[]{:S(2)}, u32[]{:S(2)}) collective-permute-start(bf16[128,768]{1,0:T(8,128)(2,1)S(1)} %broadcast_select_fusion), channel_id=1, source_target_pairs={{0,2},{1,3},{2,0},{3,1},{4,5},{5,4},{6,7},{7,6},{8,10},{9,11},{10,... | collective-permute-start | bytes 589832 | tf_op jit(solution)/shard_map/ppermute | solution.py:23
  20.6 0.9 %copy-start.2 = (bf16[128,768]{1,0:T(8,128)(2,1)S(1)}, bf16[128,768]{1,0:T(8,128)(2,1)}, u32[]{:S(2)}) copy-start(bf16[128,768]{1,0:T(8,128)(2,1)} %param.5) | copy-start | bytes 589828
  21.5 3.7 %collective-permute-start.26 = (bf16[128,768]{1,0:T(8,128)(2,1)S(1)}, bf16[128,768]{1,0:T(8,128)(2,1)S(1)}, u32[]{:S(2)}, u32[]{:S(2)}) collective-permute-start(bf16[128,768]{1,0:T(8,128)(2,1)S(1)} %copy-done.2), channel_id=1, source_target_pairs={{0,4},{4,0},{8,12},{12,8},{16,20},{20,16},{24,28},{28,24},{1,5},{5... | collective-permute-start | bytes 589832 | tf_op jit(solution)/shard_map/ppermute | solution.py:16
  21.6 3.7 %collective-permute-start.27 = (bf16[128,768]{1,0:T(8,128)(2,1)S(1)}, bf16[128,768]{1,0:T(8,128)(2,1)S(1)}, u32[]{:S(2)}, u32[]{:S(2)}) collective-permute-start(bf16[128,768]{1,0:T(8,128)(2,1)S(1)} %collective-permute-done.15), channel_id=1, source_target_pairs={{0,4},{4,0},{8,12},{12,8},{16,20},{20,16},{24,28},{28,24},{1,5},{5... | collective-permute-start | bytes 589832 | tf_op jit(solution)/shard_map/ppermute | solution.py:16
  22.2 3.1 %collective-permute-start.28 = (bf16[128,768]{1,0:T(8,128)(2,1)S(1)}, bf16[128,768]{1,0:T(8,128)(2,1)S(1)}, u32[]{:S(2)}, u32[]{:S(2)}) collective-permute-start(bf16[128,768]{1,0:T(8,128)(2,1)S(1)} %collective-permute-done.16), channel_id=1, source_target_pairs={{0,4},{4,0},{8,12},{12,8},{16,20},{20,16},{24,28},{28,24},{1,5},{5... | collective-permute-start | bytes 589832 | tf_op jit(solution)/shard_map/ppermute | solution.py:16
  25.2 1.4 %collective-permute-start.29 = (bf16[128,768]{1,0:T(8,128)(2,1)S(1)}, bf16[128,768]{1,0:T(8,128)(2,1)S(1)}, u32[]{:S(2)}, u32[]{:S(2)}) collective-permute-start(bf16[128,768]{1,0:T(8,128)(2,1)S(1)} %collective-permute-done.17), channel_id=1, source_target_pairs={{0,4},{4,0},{8,12},{12,8},{16,20},{20,16},{24,28},{28,24},{1,5},{5... | collective-permute-start | bytes 589832 | tf_op jit(solution)/shard_map/ppermute | solution.py:16
  25.2 0.9 %copy-start = (bf16[512,768]{1,0:T(8,128)(2,1)}, bf16[512,768]{1,0:T(8,128)(2,1)S(1)}, u32[]{:S(2)}) copy-start(bf16[512,768]{1,0:T(8,128)(2,1)S(1)} %constant_dynamic-update-slice_fusion.48) | copy-start | bytes 2359300
  27.3 28.7 %collective-permute-start.30 = (f32[3,512]{1,0:T(4,128)S(1)}, f32[3,512]{1,0:T(4,128)S(1)}, u32[]{:S(2)}, u32[]{:S(2)}) collective-permute-start(f32[3,512]{1,0:T(4,128)S(1)} %get-tuple-element.102), channel_id=1, source_target_pairs={{0,4},{4,0},{8,12},{12,8},{16,20},{20,16},{24,28},{28,24},{1,5},{5... | collective-permute-start | bytes 18440 | tf_op jit(solution)/shard_map/ppermute | solution.py:16
  56.2 1.1 %copy-start.1 = (bf16[512,768]{1,0:T(8,128)(2,1)S(1)}, bf16[512,768]{1,0:T(8,128)(2,1)}, u32[]{:S(2)}) copy-start(bf16[512,768]{1,0:T(8,128)(2,1)} %copy-done) | copy-start | bytes 2359300
  58.4 7.9 %collective-permute-start.33 = (bf16[72,768]{1,0:T(8,128)(2,1)S(1)}, bf16[72,768]{1,0:T(8,128)(2,1)S(1)}, u32[]{:S(2)}, u32[]{:S(2)}) collective-permute-start(bf16[72,768]{1,0:T(8,128)(2,1)S(1)} %get-tuple-element.88), channel_id=1, source_target_pairs={{0,24},{4,28},{8,16},{12,20},{16,8},{20,12},{24,0},{28,4},{1,25},{... | collective-permute-start | bytes 331784 | tf_op jit(solution)/shard_map/ppermute | solution.py:16
  60.2 11.2 %collective-permute-start.32 = (bf16[72,768]{1,0:T(8,128)(2,1)S(1)}, bf16[72,768]{1,0:T(8,128)(2,1)S(1)}, u32[]{:S(2)}, u32[]{:S(2)}) collective-permute-start(bf16[72,768]{1,0:T(8,128)(2,1)S(1)} %get-tuple-element.87), channel_id=1, source_target_pairs={{0,16},{4,20},{8,24},{12,28},{16,0},{20,4},{24,8},{28,12},{1,17},{... | collective-permute-start | bytes 331784 | tf_op jit(solution)/shard_map/ppermute | solution.py:16
  61.0 10.4 %collective-permute-start.31 = (bf16[72,768]{1,0:T(8,128)(2,1)S(1)}, bf16[72,768]{1,0:T(8,128)(2,1)S(1)}, u32[]{:S(2)}, u32[]{:S(2)}) collective-permute-start(bf16[72,768]{1,0:T(8,128)(2,1)S(1)} %get-tuple-element.86), channel_id=1, source_target_pairs={{0,8},{4,12},{8,0},{12,4},{16,24},{20,28},{24,16},{28,20},{1,9},{5... | collective-permute-start | bytes 331784 | tf_op jit(solution)/shard_map/ppermute | solution.py:16
